TPU v7x, 256 devices: a whole 4x4x8 slice. The times are simulated.
256 devices in a mesh: band: 4 (over x_hi, core), grid: 64 (over x_lo, z, y).
Axes of the slice: x: 4 (x_hi: 2, x_lo: 2; x = x_hi * 2 + x_lo), y: 4, z: 8, core: 2. Of those that a mesh axis runs over, the one named last changes fastest.
Arguments:
- orbitals: float32 [768, 16, 16, 512], P('grid', None, None, 'band'), may hold values from -24 to 24
- potential: float32 [768, 16, 16], P('grid'), may hold values from -3 to -1
- projectors: float32 [256, 8, 13, 256], P('grid'), may hold values from -0.109375 to 0.109375
- atom_planes: int32 [256, 13], P('grid'), may hold values from 0 to 23, as said below
- kb_energy: float32 [8], replicated, may hold values from 1 to 4
Outputs:
- filtered: float32 [768, 16, 16, 512], P('grid', None, None, 'band')
- correlation_gram: float32 [512, 512], P('band')
Inputs may be any that keep to these rules, and one draw needn't show every extreme that they name: `atom_planes`: each atom's row holds 13 consecutive plane numbers; the first atom starts at plane 0 and the last atom at plane 12 - 1.
All inputs are finite; a program needn't handle non-finite values.
Results may differ from a plain program's by a relative error of at most 0.0003.
Values sent between devices are 32-bit elements; how exact they have to be, the bound alone decides.
A program may use at most 128 MiB of HBM per device.

v0:
```python
import jax
import jax.numpy as jnp
from jax import lax
from jax.sharding import PartitionSpec as P

DEGREE = 4


WEIGHTS = (
    -5369.0 / 1800.0,
    12.0 / 7.0,
    -15.0 / 56.0,
    10.0 / 189.0,
    -1.0 / 112.0,
    2.0 / 1925.0,
    -1.0 / 16632.0,
)
LOWER = -4.0
CUTOFF = 1.0
UPPER = 16.0
PRECISE = lax.Precision.HIGHEST


def padded(array, sides, width):
    for axis, dim in sides:
        peers, length = (lax.axis_size(axis), array.shape[dim])
        up = [(i, (i + 1) % peers) for i in range(peers)]
        down = [(j, i) for i, j in up]
        last = lax.slice_in_dim(array, length - width, length, axis=dim)
        initial = lax.slice_in_dim(array, 0, width, axis=dim)
        before = lax.ppermute(last, axis, up)
        after = lax.ppermute(initial, axis, down)
        array = jnp.concatenate([before, array, after], axis=dim)
    return array


def shifted(array, axis, by):
    peers = lax.axis_size(axis)
    return lax.ppermute(array, axis, [(i, (i + by) % peers) for i in range(peers)])


def filter_terms(degree):
    half_span = (UPPER - CUTOFF) / 2.0
    middle = (UPPER + CUTOFF) / 2.0
    sigma_now = half_span / (LOWER - middle)
    sigma_first = sigma_now
    scales = [sigma_now / half_span]
    recall = [0.0]
    for level in range(1, degree):
        sigma_next = 1.0 / (2.0 / sigma_first - sigma_now)
        scales.append(2.0 * sigma_next / half_span)
        recall.append(sigma_now * sigma_next)
        sigma_now = sigma_next
    return (middle, scales, recall)


def second_roll(values, along):
    summed = WEIGHTS[0] * values
    for reach in range(1, 7):
        summed = summed + WEIGHTS[reach] * (
            jnp.roll(values, reach, along) + jnp.roll(values, -reach, along)
        )
    return summed


def second_planes(widened, slab_planes):
    summed = WEIGHTS[0] * widened[6 : 6 + slab_planes]
    for reach in range(1, 7):
        summed = summed + WEIGHTS[reach] * (
            widened[6 + reach : 6 + reach + slab_planes]
            + widened[6 - reach : 6 - reach + slab_planes]
        )
    return summed


def shards(orbitals, potential, projectors, atom_planes, kb_energy):
    slab_planes = orbitals.shape[0]
    orb_here = orbitals.shape[-1]
    extent = slab_planes + 12
    atom_count = atom_planes.shape[0]
    plane_marks = (
        atom_planes[:, :, None] == jnp.arange(extent, dtype=jnp.int32)[None, None, :]
    ).astype(jnp.float32)
    projector_map = jnp.einsum("abe,apbs->apes", plane_marks, projectors, precision=PRECISE)
    map_rows = atom_count * projectors.shape[1]
    projector_map = projector_map.reshape(map_rows, -1)
    energy_col = jnp.tile(kb_energy, atom_count)[:, None]
    middle, scales, recall = filter_terms(DEGREE)
    previous = orbitals
    current = orbitals
    for level in range(DEGREE):
        widened = padded(current, (("grid", 0),), 6)
        lap = (
            second_planes(widened, slab_planes) + second_roll(current, 1) + second_roll(current, 2)
        )
        local_part = -0.5 * lap + potential[..., None] * current
        correlation = (
            jnp.dot(projector_map, widened.reshape(-1, orb_here), precision=PRECISE) * energy_col
        )
        spread = lax.dot_general(
            projector_map, correlation, (((0,), (0,)), ((), ())), precision=PRECISE
        )
        spread = spread.reshape(widened.shape)
        own_part = local_part + spread[6 : 6 + slab_planes]
        low_rim = spread[:6]
        high_rim = spread[6 + slab_planes :]
        from_below = shifted(high_rim, "grid", 1)
        from_above = shifted(low_rim, "grid", -1)
        applied = own_part.at[:6].add(from_below).at[slab_planes - 6 :].add(from_above)
        result = scales[level] * (applied - middle * current)
        if level > 0:
            result = result - recall[level] * previous
        previous = current
        current = result
    flattened = current.reshape(-1, orb_here)
    piece = lax.all_gather(current, "band", axis=3, tiled=True)
    gram_part = lax.dot_general(
        flattened, piece.reshape(-1, piece.shape[-1]), (((0,), (0,)), ((), ())), precision=PRECISE
    )
    gram_total = lax.psum(gram_part, "grid")
    cell_count = slab_planes * orbitals.shape[1] * orbitals.shape[2] * lax.axis_size("grid")
    correlation_gram = gram_total * (1.0 / cell_count)
    return (current, correlation_gram)


def solution(mesh):
    return jax.shard_map(
        shards,
        mesh=mesh,
        in_specs=(
            P("grid", None, None, "band"),
            P("grid", None, None),
            P("grid", None, None, None),
            P("grid", None),
            P(),
        ),
        out_specs=(P("grid", None, None, "band"), P("band", None)),
        check_vma=False,
    )
```

profile of v0, /device:TPU:2, one launch (start us, length us, event | category | flops | bytes accessed | tf_op | source)
XLA Modules:
  0.0 987.3 jit_solution(16665948579629088824)
XLA Ops:
  7.2 2.8 fusion.325
  11.6 6.7 collective-permute-start
  59.6 5.1 fusion.326
  69.8 6.2 collective-permute-start.3
  77.3 14.2 %fusion.105 = f32[12,16,16,128]{3,2,1,0:T(8,128)S(1)} fusion(f32[12,16,16,128]{3,2,1,0:T(8,128)S(1)} %bitcast.60, f32[18,16,16,128]{3,2,1,0:T(8,128)S(1)} %get-tuple-element.305, f32[18,16,16,128]{3,2,1,0:T(8,128)S(1)} %constant_dynamic-update-slice_fusion, f32[12,15,16,128]{3,2,1,0:T(8,128)} %get-tuple-element.301, ...), kind=kLoop, calls=%fused_computation.176 | loop fusion | flops 33423360 | bytes 61353984 | tf_op jit(solution)/shard_map/add | solution.py:104
  126.2 6.4 collective-permute-start.4
  137.3 11.2 %collective-permute-done.5 = f32[6,16,16,128]{3,2,1,0:T(8,128)S(1)} collective-permute-done((f32[6,16,16,128]{3,2,1,0:T(8,128)S(1)}, f32[6,16,16,128]{3,2,1,0:T(8,128)S(1)}, u32[]{:S(2)}, u32[]{:S(2)}) %collective-permute-start.5) | collective-permute-done | bytes 786464 | tf_op jit(solution)/shard_map/ppermute | solution.py:31
  151.2 5.1 fusion.327
  158.7 6.4 collective-permute-start.7
  165.2 20.1 %fusion.71 = f32[12,16,16,128]{3,2,1,0:T(8,128)} fusion(f32[12,16,16,128]{3,2,1,0:T(8,128)} %bitcast.61, f32[12,16,16,128]{3,2,1,0:T(8,128)S(1)} %broadcast_multiply_fusion, f32[6,16,16,128]{3,2,1,0:T(8,128)S(1)} %collective-permute-done.5, f32[6,16,16,128]{3,2,1,0:T(8,128)} %copy-done.9, f32[12,15,16,128]{3,2,1,0:T(8,128)} %get-tuple-element.251, ...), kind=kLoop, calls=%fused_computation.135 | loop fusion | flops 38928384 | bytes 47198208 | tf_op jit(solution)/shard_map/add | solution.py:104
  185.2 2.4 fusion.215
  221.4 6.6 collective-permute-start.8
  232.7 9.5 collective-permute-done.9
  244.9 5.1 fusion.328
  251.4 6.5 collective-permute-start.11
  257.9 19.8 %fusion.40 = f32[12,16,16,128]{3,2,1,0:T(8,128)} fusion(f32[12,16,16,128]{3,2,1,0:T(8,128)S(1)} %bitcast.62, f32[12,16,16,128]{3,2,1,0:T(8,128)S(1)} %multiply_subtract_fusion.2, f32[6,16,16,128]{3,2,1,0:T(8,128)S(1)} %collective-permute-done.9, f32[6,16,16,128]{3,2,1,0:T(8,128)} %copy-done.11, f32[12,15,16,128]{3,2,1,0:T(8,128)} %get-tuple-element.201, ...), kind=kLoop, calls=%fused_computation.104 | loop fusion | flops 38141952 | bytes 44052480 | tf_op jit(solution)/shard_map/add | solution.py:104
  314.6 6.4 collective-permute-start.12
  325.7 8.2 collective-permute-done.13
  336.6 5.1 fusion.329
  343.0 6.5 collective-permute-start.15
  349.5 18.8 %fusion.9 = f32[12,16,16,128]{3,2,1,0:T(8,128)S(1)} fusion(f32[12,16,16,128]{3,2,1,0:T(8,128)S(1)} %bitcast.63, f32[12,16,16,128]{3,2,1,0:T(8,128)S(1)} %multiply_subtract_fusion.1, f32[6,16,16,128]{3,2,1,0:T(8,128)S(1)} %collective-permute-done.13, f32[6,16,16,128]{3,2,1,0:T(8,128)} %copy-done.10, f32[12,15,16,128]{3,2,1,0:T(8,128)} %get-tuple-element.151, ...), kind=kLoop, calls=%fused_computation.73 | loop fusion | flops 38141952 | bytes 44052480 | tf_op jit(solution)/shard_map/add | solution.py:104
  372.6 48.1 %all-gather.2.cloned.1.call-done = f32[12,16,16,512]{3,2,1,0:T(8,128)} async-done(((f32[12,16,16,128]{3,2,1,0:T(8,128)}), f32[12,16,16,512]{3,2,1,0:T(8,128)}) %all-gather.2.cloned.1.call-update) | async-done | bytes 6291472 | tf_op jit(solution)/shard_map/all_gather | solution.py:116
  420.7 7.4 convolution_bitcast_fusion.1
  428.1 550.3 %all-reduce.2.cloned.1.call-done = f32[128,512]{1,0:T(8,128)} async-done(((f32[128,512]{1,0:T(8,128)}), f32[128,512]{1,0:T(8,128)}) %all-reduce.2.cloned.1.call-update) | async-done | bytes 262160 | tf_op jit(solution)/shard_map/psum | solution.py:120
  (195 shorter events, 187.7 us)
Async XLA Ops:
  7.2 41.4 %copy-start = (f32[4,8,13,256]{3,1,2,0:T(8,128)S(1)}, f32[4,8,13,256]{3,1,2,0:T(8,128)}, u32[]{:S(2)}) copy-start(f32[4,8,13,256]{3,1,2,0:T(8,128)} %param.23) | copy-start | bytes 1277956
  7.2 11.1 %copy-start.2 = (f32[12,16,16,128]{3,2,1,0:T(8,128)S(1)}, f32[12,16,16,128]{3,2,1,0:T(8,128)}, u32[]{:S(2)}) copy-start(f32[12,16,16,128]{3,2,1,0:T(8,128)} %param.21) | copy-start | bytes 4718596
  7.2 413.5 %all-gather.2.cloned.1.call-start = ((), (), s32[]{:S(2)}) async-start(), calls=%async_computation | async-start | bytes 7864320 | tf_op jit(solution)/shard_map/all_gather | solution.py:116
  10.0 46.1 %collective-permute-start.1 = (f32[6,16,16,128]{3,2,1,0:T(8,128)}, f32[6,16,16,128]{3,2,1,0:T(8,128)}, u32[]{:S(2)}, u32[]{:S(2)}) collective-permute-start(f32[6,16,16,128]{3,2,1,0:T(8,128)} %get-tuple-element.306), channel_id=1, source_target_pairs={{0,1},{1,2},{2,3},{3,4},{4,5},{5,6},{6,7},{7,8},{8,9},{9,10},{10,1... | collective-permute-start | bytes 2359304 | tf_op jit(solution)/shard_map/ppermute | solution.py:31
  11.6 44.6 %collective-permute-start = (f32[6,16,16,128]{3,2,1,0:T(8,128)}, f32[6,16,16,128]{3,2,1,0:T(8,128)}, u32[]{:S(2)}, u32[]{:S(2)}) collective-permute-start(f32[6,16,16,128]{3,2,1,0:T(8,128)} %get-tuple-element.307), channel_id=1, source_target_pairs={{1,0},{2,1},{3,2},{4,3},{5,4},{6,5},{7,6},{8,7},{9,8},{10,9},{11,1... | collective-permute-start | bytes 2359304 | tf_op jit(solution)/shard_map/ppermute | solution.py:32
  67.6 9.6 copy-start.12
  67.6 9.6 copy-start.13
  69.7 23.6 %collective-permute-start.2 = (f32[6,16,16,128]{3,2,1,0:T(8,128)}, f32[6,16,16,128]{3,2,1,0:T(8,128)}, u32[]{:S(2)}, u32[]{:S(2)}) collective-permute-start(f32[6,16,16,128]{3,2,1,0:T(8,128)} %bitcast.5), channel_id=1, source_target_pairs={{0,1},{1,2},{2,3},{3,4},{4,5},{5,6},{6,7},{7,8},{8,9},{9,10},{10,1... | collective-permute-start | bytes 2359304 | tf_op jit(solution)/shard_map/ppermute | solution.py:39
  69.8 24.9 %collective-permute-start.3 = (f32[6,16,16,128]{3,2,1,0:T(8,128)}, f32[6,16,16,128]{3,2,1,0:T(8,128)}, u32[]{:S(2)}, u32[]{:S(2)}) collective-permute-start(f32[6,16,16,128]{3,2,1,0:T(8,128)} %bitcast.6), channel_id=1, source_target_pairs={{0,63},{1,0},{2,1},{3,2},{4,3},{5,4},{6,5},{7,6},{8,7},{9,8},{10,9... | collective-permute-start | bytes 2359304 | tf_op jit(solution)/shard_map/ppermute | solution.py:39
  126.2 22.3 %collective-permute-start.5 = (f32[6,16,16,128]{3,2,1,0:T(8,128)S(1)}, f32[6,16,16,128]{3,2,1,0:T(8,128)S(1)}, u32[]{:S(2)}, u32[]{:S(2)}) collective-permute-start(f32[6,16,16,128]{3,2,1,0:T(8,128)S(1)} %get-tuple-element.254), channel_id=1, source_target_pairs={{0,1},{1,2},{2,3},{3,4},{4,5},{5,6},{6,7},{7,8},{8,9},{9,10},{10,1... | collective-permute-start | bytes 2359304 | tf_op jit(solution)/shard_map/ppermute | solution.py:31
  126.2 22.3 %collective-permute-start.4 = (f32[6,16,16,128]{3,2,1,0:T(8,128)S(1)}, f32[6,16,16,128]{3,2,1,0:T(8,128)S(1)}, u32[]{:S(2)}, u32[]{:S(2)}) collective-permute-start(f32[6,16,16,128]{3,2,1,0:T(8,128)S(1)} %get-tuple-element.255), channel_id=1, source_target_pairs={{1,0},{2,1},{3,2},{4,3},{5,4},{6,5},{7,6},{8,7},{9,8},{10,9},{11,1... | collective-permute-start | bytes 2359304 | tf_op jit(solution)/shard_map/ppermute | solution.py:32
  158.7 26.5 %collective-permute-start.6 = (f32[6,16,16,128]{3,2,1,0:T(8,128)}, f32[6,16,16,128]{3,2,1,0:T(8,128)}, u32[]{:S(2)}, u32[]{:S(2)}) collective-permute-start(f32[6,16,16,128]{3,2,1,0:T(8,128)} %bitcast.9), channel_id=1, source_target_pairs={{0,1},{1,2},{2,3},{3,4},{4,5},{5,6},{6,7},{7,8},{8,9},{9,10},{10,1... | collective-permute-start | bytes 2359304 | tf_op jit(solution)/shard_map/ppermute | solution.py:39
  158.7 28.9 %collective-permute-start.7 = (f32[6,16,16,128]{3,2,1,0:T(8,128)}, f32[6,16,16,128]{3,2,1,0:T(8,128)}, u32[]{:S(2)}, u32[]{:S(2)}) collective-permute-start(f32[6,16,16,128]{3,2,1,0:T(8,128)} %bitcast.10), channel_id=1, source_target_pairs={{0,63},{1,0},{2,1},{3,2},{4,3},{5,4},{6,5},{7,6},{8,7},{9,8},{10,9... | collective-permute-start | bytes 2359304 | tf_op jit(solution)/shard_map/ppermute | solution.py:39
  221.4 20.8 %collective-permute-start.9 = (f32[6,16,16,128]{3,2,1,0:T(8,128)S(1)}, f32[6,16,16,128]{3,2,1,0:T(8,128)S(1)}, u32[]{:S(2)}, u32[]{:S(2)}) collective-permute-start(f32[6,16,16,128]{3,2,1,0:T(8,128)S(1)} %get-tuple-element.204), channel_id=1, source_target_pairs={{0,1},{1,2},{2,3},{3,4},{4,5},{5,6},{6,7},{7,8},{8,9},{9,10},{10,1... | collective-permute-start | bytes 2359304 | tf_op jit(solution)/shard_map/ppermute | solution.py:31
  221.4 20.8 %collective-permute-start.8 = (f32[6,16,16,128]{3,2,1,0:T(8,128)S(1)}, f32[6,16,16,128]{3,2,1,0:T(8,128)S(1)}, u32[]{:S(2)}, u32[]{:S(2)}) collective-permute-start(f32[6,16,16,128]{3,2,1,0:T(8,128)S(1)} %get-tuple-element.205), channel_id=1, source_target_pairs={{1,0},{2,1},{3,2},{4,3},{5,4},{6,5},{7,6},{8,7},{9,8},{10,9},{11,1... | collective-permute-start | bytes 2359304 | tf_op jit(solution)/shard_map/ppermute | solution.py:32
  251.4 26.3 %collective-permute-start.10 = (f32[6,16,16,128]{3,2,1,0:T(8,128)}, f32[6,16,16,128]{3,2,1,0:T(8,128)}, u32[]{:S(2)}, u32[]{:S(2)}) collective-permute-start(f32[6,16,16,128]{3,2,1,0:T(8,128)} %bitcast.13), channel_id=1, source_target_pairs={{0,1},{1,2},{2,3},{3,4},{4,5},{5,6},{6,7},{7,8},{8,9},{9,10},{10,1... | collective-permute-start | bytes 2359304 | tf_op jit(solution)/shard_map/ppermute | solution.py:39
  251.4 28.7 %collective-permute-start.11 = (f32[6,16,16,128]{3,2,1,0:T(8,128)}, f32[6,16,16,128]{3,2,1,0:T(8,128)}, u32[]{:S(2)}, u32[]{:S(2)}) collective-permute-start(f32[6,16,16,128]{3,2,1,0:T(8,128)} %bitcast.14), channel_id=1, source_target_pairs={{0,63},{1,0},{2,1},{3,2},{4,3},{5,4},{6,5},{7,6},{8,7},{9,8},{10,9... | collective-permute-start | bytes 2359304 | tf_op jit(solution)/shard_map/ppermute | solution.py:39
  314.6 19.3 %collective-permute-start.13 = (f32[6,16,16,128]{3,2,1,0:T(8,128)S(1)}, f32[6,16,16,128]{3,2,1,0:T(8,128)S(1)}, u32[]{:S(2)}, u32[]{:S(2)}) collective-permute-start(f32[6,16,16,128]{3,2,1,0:T(8,128)S(1)} %get-tuple-element.154), channel_id=1, source_target_pairs={{0,1},{1,2},{2,3},{3,4},{4,5},{5,6},{6,7},{7,8},{8,9},{9,10},{10,1... | collective-permute-start | bytes 2359304 | tf_op jit(solution)/shard_map/ppermute | solution.py:31
  314.6 19.3 %collective-permute-start.12 = (f32[6,16,16,128]{3,2,1,0:T(8,128)S(1)}, f32[6,16,16,128]{3,2,1,0:T(8,128)S(1)}, u32[]{:S(2)}, u32[]{:S(2)}) collective-permute-start(f32[6,16,16,128]{3,2,1,0:T(8,128)S(1)} %get-tuple-element.155), channel_id=1, source_target_pairs={{1,0},{2,1},{3,2},{4,3},{5,4},{6,5},{7,6},{8,7},{9,8},{10,9},{11,1... | collective-permute-start | bytes 2359304 | tf_op jit(solution)/shard_map/ppermute | solution.py:32
  343.0 25.3 %collective-permute-start.14 = (f32[6,16,16,128]{3,2,1,0:T(8,128)}, f32[6,16,16,128]{3,2,1,0:T(8,128)}, u32[]{:S(2)}, u32[]{:S(2)}) collective-permute-start(f32[6,16,16,128]{3,2,1,0:T(8,128)} %bitcast.17), channel_id=1, source_target_pairs={{0,1},{1,2},{2,3},{3,4},{4,5},{5,6},{6,7},{7,8},{8,9},{9,10},{10,1... | collective-permute-start | bytes 2359304 | tf_op jit(solution)/shard_map/ppermute | solution.py:39
  343.0 26.6 %collective-permute-start.15 = (f32[6,16,16,128]{3,2,1,0:T(8,128)}, f32[6,16,16,128]{3,2,1,0:T(8,128)}, u32[]{:S(2)}, u32[]{:S(2)}) collective-permute-start(f32[6,16,16,128]{3,2,1,0:T(8,128)} %bitcast.18), channel_id=1, source_target_pairs={{0,63},{1,0},{2,1},{3,2},{4,3},{5,4},{6,5},{7,6},{8,7},{9,8},{10,9... | collective-permute-start | bytes 2359304 | tf_op jit(solution)/shard_map/ppermute | solution.py:39
  372.5 48.2 %copy-start.3 = (f32[12,16,16,128]{3,2,1,0:T(8,128)S(1)}, f32[12,16,16,128]{3,2,1,0:T(8,128)}, u32[]{:S(2)}) copy-start(f32[12,16,16,128]{3,2,1,0:T(8,128)} %multiply_subtract_fusion) | copy-start | bytes 4718596
  372.5 605.8 %all-reduce.2.cloned.1.call-start = ((), (), s32[]{:S(2)}) async-start(), calls=%async_computation.1 | async-start | bytes 524288 | tf_op jit(solution)/shard_map/psum | solution.py:120
  420.7 559.3 %copy-start.1 = (f32[4,8,13,256]{3,1,2,0:T(8,128)S(1)}, f32[4,8,13,256]{3,1,2,0:T(8,128)}, u32[]{:S(2)}) copy-start(f32[4,8,13,256]{3,1,2,0:T(8,128)} %param.23) | copy-start | bytes 1277956
  (12 other events, 54.7 us)
Sparse Core Ops, SparseCore 0:
  372.6 47.9 all-gather.1
  428.2 550.0 all-reduce.1
where the time goes:
time: 998 us; the launch traced here: 987 us
  waiting for transfers between devices  629 us (63%)
  local copies, waits for them, and re-layouts  155 us (16%)
  other arithmetic  98.3 us (10%)
  starting transfers between devices  53.5 us (5%)
  matrix products  36.1 us (4%)
  between operations  14.9 us (1%)
    psum x1, waiting for transfers between devices, shards(): gram_total = lax.psum(gram_part, 'grid')  550 us
    slice x96, local copies, waits for them, and re-layouts, second_roll(): jnp.roll(values, -reach, along)  137 us
    add x4, other arithmetic, shards(): own_part = local_part + spread[6:6 + slab_planes]  72.9 us
    all_gather x1, waiting for transfers between devices, shards(): piece = lax.all_gather(current, 'band', axis=3, tiled=True)  48.1 us
    ppermute x4, waiting for transfers between devices, padded(): before = lax.ppermute(last, axis, up)  28.9 us
    ppermute x4, starting transfers between devices, padded(): after = lax.ppermute(initial, axis, down)  26.2 us
    ppermute x8, starting transfers between devices, shifted(): lax.ppermute(array, axis, [(i, (i + by) % peers) for i in range(peers)])  25.7 us
    dot_general x4, matrix products, shards(): lax.dot_general(projector_map, correlation, (((0,), (0,)), ((), ())), pre...  20.3 us
  transfers between devices with their start and end apart: 18, of which 6 were waited for; matrix products, arithmetic and copies ran while one was open for 14% of the time, Pallas kernels for 0%

commit v1 on v0

v1 whole, which is shorter than its diff:
```python
import functools

import jax
import jax.numpy as jnp
import ml_dtypes
import numpy as np
from jax import lax
from jax.experimental import pallas as pl
from jax.experimental.pallas import tpu as pltpu
from jax.sharding import PartitionSpec as P

DEGREE = 4
CX = 12
ROWS = 256
ORB = 128
QR = 64
NPROJ = 32
CELLS = 196608
CH_IN = 3
CH_OUT = 4
WEIGHTS = (
    -5369.0 / 1800.0,
    12.0 / 7.0,
    -15.0 / 56.0,
    10.0 / 189.0,
    -1.0 / 112.0,
    2.0 / 1925.0,
    -1.0 / 16632.0,
)
HALFW = tuple(-0.5 * w for w in WEIGHTS)
LOWER = -4.0
CUTOFF = 1.0
UPPER = 16.0
F32 = jnp.float32
BF16 = jnp.bfloat16
MESH = pl.DeviceIdType.MESH


def filter_terms(degree):
    half_span = (UPPER - CUTOFF) / 2.0
    middle = (UPPER + CUTOFF) / 2.0
    sigma_now = half_span / (LOWER - middle)
    sigma_first = sigma_now
    scales = [sigma_now / half_span]
    recall = [0.0]
    for level in range(1, degree):
        sigma_next = 1.0 / (2.0 / sigma_first - sigma_now)
        scales.append(2.0 * sigma_next / half_span)
        recall.append(sigma_now * sigma_next)
        sigma_now = sigma_next
    return middle, scales, recall


def plane_laplacian():
    mat = np.zeros((16, 16, 16, 16), np.float64)
    for a in range(16):
        for b in range(16):
            for r in range(1, 7):
                for sign in (-1, 1):
                    mat[a, b, (a + sign * r) % 16, b] += HALFW[r]
                    mat[a, b, a, (b + sign * r) % 16] += HALFW[r]
    mat = mat.reshape(256, 256).astype(np.float32)
    high = mat.astype(ml_dtypes.bfloat16)
    low = (mat - high.astype(np.float32)).astype(ml_dtypes.bfloat16)
    return np.stack([high, low])


def split(value):
    high = value.astype(BF16)
    return high, (value - high.astype(F32)).astype(BF16)


def dot(a, b):
    return jnp.dot(a, b, preferred_element_type=F32)


def dot3(a_high, a_low, b_high, b_low):
    return dot(a_high, b_high) + (dot(a_high, b_low) + dot(a_low, b_high))


def dot_t(a, b):
    return lax.dot_general(a, b, (((0,), (0,)), ((), ())), preferred_element_type=F32)


def lane_block(rows):
    return lax.broadcasted_iota(jnp.int32, (rows, ORB), 1) // 32


def roll(value, blocks):
    blocks = blocks % 4
    return value if blocks == 0 else pltpu.roll(value, 32 * blocks, 1)


def transpose_blocks(parts):
    blk = lane_block(parts[0].shape[0])
    low = blk < 2
    even = (blk % 2) == 0
    a0, a1, a2, a3 = parts
    b0 = jnp.where(low, a0, roll(a2, 2))
    b2 = jnp.where(low, roll(a0, 2), a2)
    b1 = jnp.where(low, a1, roll(a3, 2))
    b3 = jnp.where(low, roll(a1, 2), a3)
    return (
        jnp.where(even, b0, roll(b1, 1)),
        jnp.where(even, roll(b0, 3), b1),
        jnp.where(even, b2, roll(b3, 1)),
        jnp.where(even, roll(b2, 3), b3),
    )


def loop(start, stop, body):
    lax.fori_loop(start, stop, lambda i, c: (body(i), c)[1], 0)


def kernel(
    orb, pot, payload, kbt, lap, out, gram,
    x_in, r_in, pg, potg, cm, rim, chi_h, chi_l, cht_h, cht_l, pc_mat, wide, base_lv,
    halo_s, halo_r, part, pc_s, pc_r, cc_h, cc_l, fix,
    x_out, r_out, filt, filt_c, xr, xr2, gb, yr, sb, sr, st, xt, tb, go,
    in_s, in_r, chi_s, chi_r, cor_s, cor_r, pot_s, pot_r, rim_s, rim_r, hal_s, hal_r, par_s, par_r,
    out_s, out_r, fc_s, fc_r, xs_s, xs_r, rl_s, rl_r, ys_s, ys_r, ss_s, ss_r, xh_s, xh_r, sg_s, sg_r, yg_s, yg_r, loc, hbm,
):
    middle, scales, recall = filter_terms(DEGREE)
    b = lax.axis_index("band")
    g = lax.axis_index("grid")
    s, y = g // 4, g % 4
    xh, c = b // 2, b % 2
    core = (2 * xh + 1 - c, g)
    across = (2 * (1 - xh) + c, g)
    cross = (2 * (1 - xh) + 1 - c, g)
    up = (b, (g + 4) % 64)
    down = (b, (g + 60) % 64)
    ypeer = [None] + [(b, 4 * s + (y + k) % 4) for k in range(1, 4)]
    speer = [None] + [(b, (g + 4 * d) % 64) for d in range(1, 16)]
    pending = []

    def rcopy(src, dst, ssem, rsem, dev):
        cp = pltpu.make_async_remote_copy(
            src_ref=src, dst_ref=dst, send_sem=ssem, recv_sem=rsem, device_id=dev, device_id_type=MESH
        )
        cp.start()
        pending.append(cp)
        return cp

    barrier = pltpu.get_barrier_semaphore()
    friends = ypeer[1:] + speer[1:] + [core, across, cross]
    for dev in friends:
        pl.semaphore_signal(barrier, inc=1, device_id=dev, device_id_type=MESH)
    pl.semaphore_wait(barrier, len(friends))

    half = pl.ds(27 * c, 27)
    chi_in = [None]
    pot_in = [None]
    for k in range(1, 4):
        chi_in.append(rcopy(payload.at[half], pg.at[y, half], chi_s.at[k - 1], chi_r.at[k - 1], ypeer[k]))
        pot_in.append(rcopy(pot, potg.at[y], pot_s.at[k - 1], pot_r.at[k - 1], ypeer[k]))
    own_pg = pltpu.make_async_copy(payload, pg.at[y], loc.at[0])
    own_pg.start()
    own_pot = pltpu.make_async_copy(pot, potg.at[y], loc.at[1])
    own_pot.start()

    span = CX // CH_IN
    orb_in = []
    orb_own = []

    def pack_in(i):
        parts = [orb[i, pl.ds(QR * q, QR), :] for q in range(4)]
        for k, value in enumerate(transpose_blocks(parts)):
            x_in[k, i] = value

    for ch in range(CH_IN):
        loop(span * ch, span * (ch + 1), pack_in)
        planes = pl.ds(span * ch, span)
        row = []
        for k in range(1, 4):
            row.append(
                rcopy(
                    x_in.at[(y + k) % 4, planes], r_in.at[y, planes],
                    in_s.at[k - 1, ch], in_r.at[k - 1, ch], ypeer[k],
                )
            )
        orb_in.append(row)
        own = pltpu.make_async_copy(x_in.at[y, planes], r_in.at[y, planes], loc.at[2 + ch])
        own.start()
        orb_own.append(own)

    for slot in range(4, 8):
        potg[slot] = jnp.zeros((16, ROWS), F32)
    own_pot.wait()
    for k in range(1, 4):
        pot_in[k].wait_recv()
    pot_t = potg[...].reshape(128, ROWS).T
    p_high = pot_t.astype(BF16)
    rest = pot_t - p_high.astype(F32)
    p_mid = rest.astype(BF16)
    p_low = (rest - p_mid.astype(F32)).astype(BF16)
    centre = 3.0 * HALFW[0] - middle
    e_row = lax.broadcasted_iota(jnp.int32, (128, ORB), 0)
    e_same = (e_row // 16) == lane_block(128)

    def spread_pot(i):
        pick = jnp.where(e_same & (e_row % 16 == i), 1.0, 0.0).astype(BF16)
        pc_mat[i] = (dot(p_high, pick) + (dot(p_mid, pick) + dot(p_low, pick))) + centre

    loop(0, CX, spread_pot)

    cor_in = [None]
    own_pg.wait()
    for k in range(1, 4):
        chi_in[k].wait_recv()
        src = (y + 4 - k) % 4
        cor_in.append(rcopy(pg.at[src, half], pg.at[src, half], cor_s.at[k - 1], cor_r.at[k - 1], core))
    for k in range(1, 4):
        cor_in[k].wait_recv()

    def place(dom):
        for j in range(4):
            start = pg[dom, 52 + j // 2, :, pl.ds(128 * (j % 2), 128)]
            bits = {}
            left = start
            for size in (8, 4, 2, 1):
                bits[size] = left >= (size - 0.5)
                left = jnp.where(bits[size], left - size, left)
            for lh in range(2):
                lanes = pl.ds(128 * lh, 128)
                zero = jnp.zeros((8, 128), F32)
                rows = [pg[dom, 13 * j + n, :, lanes] for n in range(13)]
                for size in (1, 2, 4, 8):
                    count = min(len(rows) + size, 24)
                    at = lambda n, rows=rows: rows[n] if 0 <= n < len(rows) else zero
                    rows = [jnp.where(bits[size], at(n - size), at(n)) for n in range(count)]
                for n in range(24):
                    cm[dom, n, pl.ds(8 * j, 8), lanes] = rows[n]

    loop(0, 4, place)
    rim_in = [
        rcopy(cm.at[3, pl.ds(18, 6)], rim.at[0], rim_s.at[0], rim_r.at[0], up),
        rcopy(cm.at[0, pl.ds(0, 6)], rim.at[1], rim_s.at[1], rim_r.at[1], down),
    ]
    for cp in rim_in:
        cp.wait_recv()

    def make_chi(i, beside):
        mat = jnp.concatenate([cm[d, i + 6] for d in range(4)] + beside, axis=0)
        chi_h[i], chi_l[i] = split(mat)
        cht_h[i], cht_l[i] = split(mat.T)

    loop(0, 6, lambda i: make_chi(i, [rim[0, i]] + [cm[d, i + 18] for d in range(3)]))
    loop(6, 12, lambda i: make_chi(i, [cm[d, i - 6] for d in range(1, 4)] + [rim[1, i - 6]]))

    def unpack_in(i):
        parts = [r_in[m, i] for m in range(4)]
        for q, value in enumerate(transpose_blocks(parts)):
            wide[0, 6 + i, pl.ds(QR * q, QR), :] = value
            wide[1, 6 + i, pl.ds(QR * q, QR), :] = value

    for ch in range(CH_IN):
        orb_own[ch].wait()
        for cp in orb_in[ch]:
            cp.wait_recv()
        loop(span * ch, span * (ch + 1), unpack_in)

    blk64 = lane_block(QR)
    blk32 = lane_block(NPROJ)
    for lv in range(DEGREE):
        cur, nxt = lv % 2, 1 - lv % 2
        scale, back = scales[lv], recall[lv]

        def pack_halo(i):
            high = jnp.zeros((QR, ORB), F32)
            low = jnp.zeros((QR, ORB), F32)
            for q in range(4):
                high = jnp.where(blk64 == q, roll(wide[cur, 12 + i, pl.ds(QR * q, QR), :], q - 3), high)
                low = jnp.where(blk64 == q, roll(wide[cur, 6 + i, pl.ds(QR * q, QR), :], q), low)
            halo_s[lv, 0, i] = high
            halo_s[lv, 1, i] = low

        loop(0, 6, pack_halo)
        halo_in = [
            rcopy(halo_s.at[lv, 0], halo_r.at[lv, 0], hal_s.at[lv, 0], hal_r.at[lv, 0], up),
            rcopy(halo_s.at[lv, 1], halo_r.at[lv, 1], hal_s.at[lv, 1], hal_r.at[lv, 1], down),
        ]

        def rims(i):
            for q in range(4):
                rows = pl.ds(QR * q, QR)
                wide[cur, i, rows, :] = jnp.where(blk64 == 0, 0.0, roll(wide[cur, 12 + i, rows, :], 1))
                wide[cur, 18 + i, rows, :] = jnp.where(blk64 == 3, 0.0, roll(wide[cur, 6 + i, rows, :], 3))

        loop(0, 6, rims)
        part[...] = jnp.zeros_like(part)

        def local(i):
            high, low = split(wide[cur, 6 + i])
            partial = dot3(chi_h[i], chi_l[i], high, low)
            part[0] += partial[:128]
            part[1 + i // 6] += partial[128:]
            base_lv[...] = dot3(lap[0], lap[1], high, low)
            for q in range(4):
                rows = pl.ds(QR * q, QR)
                value = base_lv[rows, :] + pc_mat[i, rows, :] * wide[cur, 6 + i, rows, :]
                for r in range(1, 7):
                    value = value + HALFW[r] * (wide[cur, 6 + i + r, rows, :] + wide[cur, 6 + i - r, rows, :])
                value = scale * value
                if lv > 0:
                    value = value - back * wide[nxt, 6 + i, rows, :]
                wide[nxt, 6 + i, rows, :] = value

        loop(0, CX, local)
        for n in range(3):
            packed = jnp.zeros((NPROJ, ORB), F32)
            for d in range(4):
                packed = jnp.where(blk32 == d, part[n, pl.ds(NPROJ * d, NPROJ), :], packed)
            pc_s[lv, n] = packed
        part_in = [
            rcopy(pc_s.at[lv], pc_r.at[lv, 0], par_s.at[lv, 0], par_r.at[lv, 0], up),
            rcopy(pc_s.at[lv], pc_r.at[lv, 1], par_s.at[lv, 1], par_r.at[lv, 1], down),
        ]
        for cp in halo_in:
            cp.wait_recv()

        for i in range(6):
            low = HALFW[i + 1] * halo_r[lv, 0, 5]
            for r in range(i + 2, 7):
                low = low + HALFW[r] * halo_r[lv, 0, 6 + i - r]
            fix[i] = low
            high = HALFW[6 - i] * halo_r[lv, 1, 0]
            for r in range(7 - i, 7):
                high = high + HALFW[r] * halo_r[lv, 1, i + r - 6]
            fix[6 + i] = high
        for cp in part_in:
            cp.wait_recv()
        own, dn, hi = pc_s[lv, 0], pc_s[lv, 1], pc_s[lv, 2]
        corr = (
            own
            + jnp.where(blk32 == 0, roll(pc_r[lv, 0, 2], 1), roll(hi, 1))
            + jnp.where(blk32 == 3, roll(pc_r[lv, 1, 1], 3), roll(dn, 3))
        )
        corr_low = roll(pc_r[lv, 0, 0], 1) + roll(pc_r[lv, 0, 2], 2) + dn
        corr_high = roll(pc_r[lv, 1, 0], 3) + roll(pc_r[lv, 1, 1], 2) + hi
        beside_low = jnp.where(blk32 == 0, corr_low, roll(corr, 1))
        beside_high = jnp.where(blk32 == 3, corr_high, roll(corr, 3))
        energy = jnp.concatenate([kbt[...]] * 4, axis=0) * scale
        for n, value in enumerate((corr, beside_low, beside_high)):
            high, low = split(value * energy)
            high, low = high.astype(F32), low.astype(F32)
            for d in range(4):
                rows = pl.ds(NPROJ * d, NPROJ)
                cc_h[n, rows, :] = jnp.where(blk32 == d, high, 0.0).astype(BF16)
                cc_l[n, rows, :] = jnp.where(blk32 == d, low, 0.0).astype(BF16)

        def finish(i, n, edge):
            ch = jnp.concatenate([cc_h[0], cc_h[n]], axis=0)
            cl = jnp.concatenate([cc_l[0], cc_l[n]], axis=0)
            base_lv[...] = dot3(cht_h[i], cht_l[i], ch, cl)
            for q in range(4):
                rows = pl.ds(QR * q, QR)
                more = jnp.where(blk64 == edge, roll(fix[i], edge - q), 0.0)
                wide[nxt, 6 + i, rows, :] = wide[nxt, 6 + i, rows, :] + (base_lv[rows, :] + scale * more)

        loop(0, 6, lambda i: finish(i, 1, 0))
        loop(6, 12, lambda i: finish(i, 2, 3))

    last = DEGREE % 2

    def pack_out(i):
        parts = [wide[last, 6 + i, pl.ds(QR * q, QR), :] for q in range(4)]
        for k, value in enumerate(transpose_blocks(parts)):
            x_out[k, i] = value

    def first_plane(ch):
        return (6 * (1 - xh) if ch < 2 else 6 * xh) + 3 * (ch % 2)

    back_in = []
    back_own = []
    for ch in range(CH_OUT):
        first = first_plane(ch)
        loop(0, 3, lambda i: pack_out(first + i))
        planes = pl.ds(first, 3)
        row = []
        for k in range(1, 4):
            row.append(
                rcopy(
                    x_out.at[(y + k) % 4, planes], r_out.at[y, planes],
                    out_s.at[k - 1, ch], out_r.at[k - 1, ch], ypeer[k],
                )
            )
        back_in.append(row)
        own = pltpu.make_async_copy(x_out.at[y, planes], r_out.at[y, planes], loc.at[8 + ch])
        own.start()
        back_own.append(own)

    def unpack_out(i):
        parts = [r_out[m, i] for m in range(4)]
        for q, value in enumerate(transpose_blocks(parts)):
            filt[i, pl.ds(QR * q, QR), :] = value

    fc_in = []
    x_recv = []
    stores = []
    for ch in range(CH_OUT):
        first = first_plane(ch)
        back_own[ch].wait()
        for cp in back_in[ch]:
            cp.wait_recv()
        loop(0, 3, lambda i: unpack_out(first + i))
        planes = pl.ds(first, 3)
        if ch < 2:
            x_recv.append(rcopy(filt.at[planes], xr.at[pl.ds(3 * ch, 3)], xs_s.at[ch], xs_r.at[ch], across))
        fc_in.append(rcopy(filt.at[planes], filt_c.at[planes], fc_s.at[ch], fc_r.at[ch], core))
        store = pltpu.make_async_copy(filt.at[planes], out.at[planes], hbm.at[ch])
        store.start()
        stores.append(store)

    gb[...] = jnp.zeros_like(gb)

    def gram_step(slot, lhs, rhs):
        a_high, a_low = split(lhs)
        parts = [split(value) for value in rhs]
        r_high = jnp.concatenate([p[0] for p in parts], axis=1)
        r_low = jnp.concatenate([p[1] for p in parts], axis=1)
        value = dot_t(a_high, r_high) + (dot_t(a_high, r_low) + dot_t(a_low, r_high))
        gb[slot] += value[:, :128]
        gb[slot + 1] += value[:, 128:]

    for cp in fc_in:
        cp.wait_recv()
    loop(0, CX, lambda i: gram_step(0, filt[i], [filt[i], filt_c[i]]))
    relay = []
    for ch in range(2):
        x_recv[ch].wait_recv()
        planes = pl.ds(3 * ch, 3)
        relay.append(rcopy(xr.at[planes], xr2.at[planes], rl_s.at[ch], rl_r.at[ch], core))
    for ch in range(2):
        relay[ch].wait_recv()
        loop(3 * ch, 3 * ch + 3, lambda i: gram_step(2, filt[6 * xh + i], [xr[i], xr2[i]]))
    for n in (2, 3):
        gb[n] = jnp.where(xh == 1, gb[n].T, gb[n])

    y_in = []
    for k in range(1, 4):
        y_in.append(rcopy(gb.at[(y + k) % 4], yr.at[k - 1], ys_s.at[k - 1], ys_r.at[k - 1], ypeer[k]))
    for cp in y_in:
        cp.wait_recv()
    sb[...] = (gb[y] + (yr[0] + (yr[1] + yr[2]))).reshape(16, 8, 128)
    for d in range(1, 16):
        cp = pltpu.make_async_remote_copy(
            src_ref=sb.at[(s + d) % 16], dst_ref=sr.at[d - 1], send_sem=ss_s, recv_sem=ss_r,
            device_id=speer[d], device_id_type=MESH,
        )
        cp.start()
    pltpu.make_async_copy(sr, sr, ss_r).wait()
    tile = sb[s]
    for d in range(15):
        tile = tile + sr[d]
    st[...] = tile
    partner = (2 * (1 - xh) + (c + y // 3 * (1 - 2 * c)), g)
    xh_in = rcopy(st, xt, xh_s.at[0], xh_r.at[0], partner)
    xh_in.wait_recv()
    tb[s] = tile + jnp.where(y >= 2, xt[...], 0.0)
    for d in range(1, 16):
        cp = pltpu.make_async_remote_copy(
            src_ref=tb.at[s], dst_ref=tb.at[s], send_sem=sg_s, recv_sem=sg_r,
            device_id=speer[d], device_id_type=MESH,
        )
        cp.start()
    pltpu.make_async_copy(sr, sr, sg_r).wait()
    go[y] = tb[...].reshape(128, 128) * (1.0 / CELLS)
    yg_in = []
    for k in range(1, 4):
        yg_in.append(rcopy(go.at[y], go.at[y], yg_s.at[k - 1], yg_r.at[k - 1], ypeer[k]))
    for cp in yg_in:
        cp.wait_recv()
    gram[b] = go[0]
    gram[core[0]] = go[1]
    gram[across[0]] = jnp.where(xh == 1, go[2].T, go[2])
    gram[cross[0]] = jnp.where(xh == 1, go[3].T, go[3])

    pltpu.make_async_copy(sr, sr, ss_s).wait()
    pltpu.make_async_copy(sr, sr, sg_s).wait()
    for cp in stores:
        cp.wait()
    for cp in pending:
        cp.wait_send()


def run(orb, pot, payload, kbt, lap):
    vmem = functools.partial(pltpu.VMEM)
    dma = pltpu.SemaphoreType.DMA
    f = lambda *shape: vmem(shape, F32)
    h = lambda *shape: vmem(shape, BF16)
    scratch = [
        f(4, CX, QR, ORB), f(4, CX, QR, ORB), f(4, 54, 8, ROWS), f(8, 16, ROWS), f(4, 24, NPROJ, ROWS),
        f(2, 6, NPROJ, ROWS), h(CX, ROWS, ROWS), h(CX, ROWS, ROWS), h(CX, ROWS, ROWS), h(CX, ROWS, ROWS),
        f(CX, ROWS, ORB), f(2, 24, ROWS, ORB), f(ROWS, ORB),
        f(DEGREE, 2, 6, QR, ORB), f(DEGREE, 2, 6, QR, ORB), f(3, 128, ORB),
        f(DEGREE, 3, NPROJ, ORB), f(DEGREE, 2, 3, NPROJ, ORB), h(3, 128, ORB), h(3, 128, ORB), f(CX, QR, ORB),
        f(4, CX, QR, ORB), f(4, CX, QR, ORB), f(CX, ROWS, ORB), f(CX, ROWS, ORB), f(6, ROWS, ORB), f(6, ROWS, ORB),
        f(4, 128, 128), f(3, 128, 128), f(16, 8, 128), f(15, 8, 128), f(8, 128), f(8, 128), f(16, 8, 128),
        f(4, 128, 128),
        dma((3, CH_IN)), dma((3, CH_IN)), dma((3,)), dma((3,)), dma((3,)), dma((3,)), dma((3,)), dma((3,)),
        dma((2,)), dma((2,)), dma((DEGREE, 2)), dma((DEGREE, 2)), dma((DEGREE, 2)), dma((DEGREE, 2)),
        dma((3, CH_OUT)), dma((3, CH_OUT)), dma((CH_OUT,)), dma((CH_OUT,)), dma((2,)), dma((2,)), dma((2,)), dma((2,)),
        dma((3,)), dma((3,)), dma, dma, dma((1,)), dma((1,)), dma, dma, dma((3,)), dma((3,)), dma((16,)), dma((CH_OUT,)),
    ]
    spec = pl.BlockSpec(memory_space=pltpu.VMEM)
    return pl.pallas_call(
        kernel,
        out_shape=(
            jax.ShapeDtypeStruct((CX, ROWS, ORB), F32),
            jax.ShapeDtypeStruct((4, 128, 128), F32),
        ),
        in_specs=[spec] * 5,
        out_specs=(pl.BlockSpec(memory_space=pl.ANY), spec),
        scratch_shapes=scratch,
        compiler_params=pltpu.CompilerParams(
            collective_id=0, has_side_effects=True, vmem_limit_bytes=60 * 2**20
        ),
        name="chebyshev",
    )(orb, pot, payload, kbt, lap)


def shards(orbitals, potential, projectors, atom_planes, kb_energy):
    pot = jnp.pad(potential.reshape(CX, ROWS), ((0, 4), (0, 0)))
    starts = jnp.broadcast_to(
        atom_planes[:, 0].astype(F32).reshape(2, 1, 2, 1), (2, 8, 2, 128)
    ).reshape(2, 8, ROWS)
    payload = jnp.concatenate([projectors.transpose(0, 2, 1, 3).reshape(52, 8, ROWS), starts], axis=0)
    kbt = jnp.broadcast_to(kb_energy[:, None], (8, ORB))
    filtered, gram = run(orbitals.reshape(CX, ROWS, ORB), pot, payload, kbt, jnp.asarray(plane_laplacian()))
    return filtered.reshape(orbitals.shape), gram.transpose(1, 0, 2).reshape(128, 512)


def solution(mesh):
    return jax.shard_map(
        shards,
        mesh=mesh,
        in_specs=(
            P("grid", None, None, "band"),
            P("grid", None, None),
            P("grid", None, None, None),
            P("grid", None),
            P(),
        ),
        out_specs=(P("grid", None, None, "band"), P("band", None)),
        check_vma=False,
    )
```

time: 998 us -> 158 us (0.16)
  waiting for transfers between devices: 629 us -> 0 us
  local copies, waits for them, and re-layouts: 155 us -> 7.65 us
  Pallas kernels: 0 us -> 146 us
  other arithmetic: 98.3 us -> 2.59 us
  starting transfers between devices: 53.5 us -> 0 us
  matrix products: 36.1 us -> 0 us
  between operations: 14.9 us -> 0.65 us
    psum x1 -> x0, waiting for transfers between devices: 550 us -> none  [shards(): gram_total = lax.psum(gram_part, 'grid')]
    slice x109 -> x0, local copies, waits for them, and re-layouts: 147 us -> none  [the longest x96 137 us: second_roll(): jnp.roll(values, -reach, along)]
    pallas_call x0 -> x1, Pallas kernels: none -> 146 us  [run(): pl.pallas_call(kernel, out_shape=(jax.ShapeDtypeStruct((CX, ROWS, ORB), F...]
    add x4 -> x0, other arithmetic: 72.9 us -> none  [shards(): own_part = local_part + spread[6:6 + slab_planes]]
    ppermute x16 -> x0, starting transfers between devices: 53.5 us -> none  [the longest x4 26.2 us: padded(): after = lax.ppermute(initial, axis, down)]
    all_gather x1 -> x0, waiting for transfers between devices: 48.1 us -> none  [shards(): piece = lax.all_gather(current, 'band', axis=3, tiled=True)]
    dot_general x10 -> x0, matrix products: 36.1 us -> none  [the longest x4 20.3 us: shards(): lax.dot_general(projector_map, correlation, (((0,), (0,)), ((), ())), pre...]
    ppermute x16 -> x0, waiting for transfers between devices: 30.7 us -> none  [the longest x4 28.9 us: padded(): before = lax.ppermute(last, axis, up)]
  transfers between devices with their start and end apart: 18 -> 0, of which waited for: 6 -> 0; matrix products, arithmetic and copies ran while one was open for 14% -> 0% of each run, Pallas kernels for 0% -> 0%
where the time goes in v1:
time: 158 us; the launch traced here: 157 us
  Pallas kernels  146 us (92%)
  local copies, waits for them, and re-layouts  7.65 us (5%)
  other arithmetic  2.59 us (2%)
    pallas_call x1, Pallas kernels, run(): pl.pallas_call(kernel, out_shape=(jax.ShapeDtypeStruct((CX, ROWS, ORB), F...  146 us
    unnamed x4, local copies, waits for them, and re-layouts  3.57 us

profile of v1, /device:TPU:2, one launch (start us, length us, event | category | flops | bytes accessed | tf_op | source)
XLA Modules:
  0.0 157.1 jit_solution(8966867197472341887)
XLA Ops:
  0.6 0.8 convert_reduce_fusion
  1.4 0.1 convert_element_type.13
  1.5 0.1 broadcast_bitcast_fusion
  1.6 1.3 broadcast_in_dim.18.kbt
  2.9 1.0 reshape.30
  3.9 0.6 pad.4.pot
  4.5 1.8 %pad_maximum_fusion.payload = f32[54,8,256]{2,1,0:T(8,128)} fusion(f32[2,8,256]{2,1,0:T(8,128)S(1)} %broadcast_in_dim.17, f32[52,8,256]{2,1,0:T(8,128)} %bitcast.15), kind=kLoop, calls=%fused_computation | loop fusion | flops 110592 | bytes 884736 | tf_op jit(solution)/shard_map/concatenate | solution.py:528
  6.3 146.2 %chebyshev.1 = (f32[12,256,128]{2,1,0:T(8,128)}, f32[4,128,128]{2,1,0:T(8,128)}) custom-call(f32[12,256,128]{2,1,0:T(8,128)} %bitcast.12, f32[16,256]{1,0:T(8,128)} %pad.4.pot, f32[54,8,256]{2,1,0:T(8,128)} %pad_maximum_fusion.payload, f32[8,128]{1,0:T(8,128)} %broadcast_in_dim.18.kbt, bf16[2,256,256]{2,1,0:T(8,128)(2,1)} %constant.5.clone.lap), custom_call_target="tpu_custom_call" | custom-call | tf_op jit(solution)/shard_map/chebyshev/pallas_call | solution.py:507
  152.5 1.1 copy.8
  153.6 0.8 copy.9
  154.4 2.7 %copy.14 = f32[12,16,16,128]{3,2,1,0:T(8,128)} copy(f32[12,16,16,128]{3,2,1,0:T(8,128)} %bitcast.13) | data formatting | bytes 3145728
  (2 shorter events, 0.0 us)

commit v2 on v1

--- a/solution.py
+++ b/solution.py
@@ -113,8 +113,8 @@
 
 
 def kernel(
-    orb, pot, payload, kbt, lap, out, gram,
-    x_in, r_in, pg, potg, cm, rim, chi_h, chi_l, cht_h, cht_l, pc_mat, wide, base_lv,
+    orb, pot, proj, planes_ref, kb, lap, out, gram,
+    flat, payload, pot_s16, x_in, r_in, pg, potg, cm, rim, chi_h, chi_l, cht_h, cht_l, pc_mat, wide, base_lv, hl,
     halo_s, halo_r, part, pc_s, pc_r, cc_h, cc_l, fix,
     x_out, r_out, filt, filt_c, xr, xr2, gb, yr, sb, sr, st, xt, tb, go,
     in_s, in_r, chi_s, chi_r, cor_s, cor_r, pot_s, pot_r, rim_s, rim_r, hal_s, hal_r, par_s, par_r,
@@ -146,6 +146,22 @@
     friends = ypeer[1:] + speer[1:] + [core, across, cross]
     for dev in friends:
         pl.semaphore_signal(barrier, inc=1, device_id=dev, device_id_type=MESH)
+
+    for j in range(4):
+        for p in range(8):
+            for lh in range(2):
+                flat[lh, pl.ds(128 * j + 16 * p, 13), :] = proj[j, p, :, pl.ds(128 * lh, 128)]
+    for j in range(4):
+        for n in range(13):
+            for lh in range(2):
+                payload[13 * j + n, :, pl.ds(128 * lh, 128)] = flat[lh, pl.ds(128 * j + n, 8, stride=16), :]
+        payload[52 + j // 2, :, pl.ds(128 * (j % 2), 128)] = jnp.full((8, 128), planes_ref[j, 0].astype(F32))
+    pot_s16[pl.ds(0, 8), :] = pot[pl.ds(0, 8), :]
+    pot_s16[pl.ds(8, 8), :] = jnp.concatenate([pot[pl.ds(8, 4), :], jnp.zeros((4, ROWS), F32)], axis=0)
+    p_row = lax.broadcasted_iota(jnp.int32, (8, ORB), 0)
+    kbt = jnp.zeros((8, ORB), F32)
+    for p in range(8):
+        kbt = jnp.where(p_row == p, kb[p], kbt)
     pl.semaphore_wait(barrier, len(friends))
 
     half = pl.ds(27 * c, 27)
@@ -153,10 +169,10 @@
     pot_in = [None]
     for k in range(1, 4):
         chi_in.append(rcopy(payload.at[half], pg.at[y, half], chi_s.at[k - 1], chi_r.at[k - 1], ypeer[k]))
-        pot_in.append(rcopy(pot, potg.at[y], pot_s.at[k - 1], pot_r.at[k - 1], ypeer[k]))
+        pot_in.append(rcopy(pot_s16, potg.at[y], pot_s.at[k - 1], pot_r.at[k - 1], ypeer[k]))
     own_pg = pltpu.make_async_copy(payload, pg.at[y], loc.at[0])
     own_pg.start()
-    own_pot = pltpu.make_async_copy(pot, potg.at[y], loc.at[1])
+    own_pot = pltpu.make_async_copy(pot_s16, potg.at[y], loc.at[1])
     own_pot.start()
 
     span = CX // CH_IN
@@ -262,51 +278,58 @@
 
     blk64 = lane_block(QR)
     blk32 = lane_block(NPROJ)
+
+    def send_halo(lv, side):
+        return rcopy(
+            halo_s.at[lv, side], halo_r.at[lv, side], hal_s.at[lv, side], hal_r.at[lv, side], (up, down)[side]
+        )
+
+    def pack_halo(i):
+        high = jnp.zeros((QR, ORB), F32)
+        low = jnp.zeros((QR, ORB), F32)
+        for q in range(4):
+            high = jnp.where(blk64 == q, roll(wide[0, 12 + i, pl.ds(QR * q, QR), :], q - 3), high)
+            low = jnp.where(blk64 == q, roll(wide[0, 6 + i, pl.ds(QR * q, QR), :], q), low)
+        halo_s[0, 0, i] = high
+        halo_s[0, 1, i] = low
+
+    back_in = []
+    back_own = []
+
+    def send_out(ch):
+        planes = pl.ds(3 * ch, 3)
+        row = []
+        for k in range(1, 4):
+            row.append(
+                rcopy(
+                    x_out.at[(y + k) % 4, planes], r_out.at[y, planes],
+                    out_s.at[k - 1, ch], out_r.at[k - 1, ch], ypeer[k],
+                )
+            )
+        back_in.append(row)
+        own = pltpu.make_async_copy(x_out.at[y, planes], r_out.at[y, planes], loc.at[8 + ch])
+        own.start()
+        back_own.append(own)
+
+    loop(0, 6, pack_halo)
+    halo_in = [send_halo(0, 0), send_halo(0, 1)]
     for lv in range(DEGREE):
         cur, nxt = lv % 2, 1 - lv % 2
         scale, back = scales[lv], recall[lv]
-
-        def pack_halo(i):
-            high = jnp.zeros((QR, ORB), F32)
-            low = jnp.zeros((QR, ORB), F32)
-            for q in range(4):
-                high = jnp.where(blk64 == q, roll(wide[cur, 12 + i, pl.ds(QR * q, QR), :], q - 3), high)
-                low = jnp.where(blk64 == q, roll(wide[cur, 6 + i, pl.ds(QR * q, QR), :], q), low)
-            halo_s[lv, 0, i] = high
-            halo_s[lv, 1, i] = low
-
-        loop(0, 6, pack_halo)
-        halo_in = [
-            rcopy(halo_s.at[lv, 0], halo_r.at[lv, 0], hal_s.at[lv, 0], hal_r.at[lv, 0], up),
-            rcopy(halo_s.at[lv, 1], halo_r.at[lv, 1], hal_s.at[lv, 1], hal_r.at[lv, 1], down),
-        ]
-
-        def rims(i):
-            for q in range(4):
-                rows = pl.ds(QR * q, QR)
-                wide[cur, i, rows, :] = jnp.where(blk64 == 0, 0.0, roll(wide[cur, 12 + i, rows, :], 1))
-                wide[cur, 18 + i, rows, :] = jnp.where(blk64 == 3, 0.0, roll(wide[cur, 6 + i, rows, :], 3))
-
-        loop(0, 6, rims)
         part[...] = jnp.zeros_like(part)
 
-        def local(i):
-            high, low = split(wide[cur, 6 + i])
-            partial = dot3(chi_h[i], chi_l[i], high, low)
-            part[0] += partial[:128]
-            part[1 + i // 6] += partial[128:]
-            base_lv[...] = dot3(lap[0], lap[1], high, low)
-            for q in range(4):
-                rows = pl.ds(QR * q, QR)
-                value = base_lv[rows, :] + pc_mat[i, rows, :] * wide[cur, 6 + i, rows, :]
-                for r in range(1, 7):
-                    value = value + HALFW[r] * (wide[cur, 6 + i + r, rows, :] + wide[cur, 6 + i - r, rows, :])
-                value = scale * value
-                if lv > 0:
-                    value = value - back * wide[nxt, 6 + i, rows, :]
-                wide[nxt, 6 + i, rows, :] = value
-
-        loop(0, CX, local)
+        def partials(i):
+            for n in range(2):
+                at = i + 6 * n
+                high, low = split(wide[cur, 6 + at])
+                hl[i, 0, :, pl.ds(ORB * n, ORB)] = high
+                hl[i, 1, :, pl.ds(ORB * n, ORB)] = low
+                both = dot(chi_h[at], jnp.concatenate([high, low], axis=1))
+                value = both[:, :ORB] + (both[:, ORB:] + dot(chi_l[at], high))
+                part[0] += value[:128]
+                part[1 + n] += value[128:]
+
+        loop(0, 6, partials)
         for n in range(3):
             packed = jnp.zeros((NPROJ, ORB), F32)
             for d in range(4):
@@ -316,6 +339,30 @@
             rcopy(pc_s.at[lv], pc_r.at[lv, 0], par_s.at[lv, 0], par_r.at[lv, 0], up),
             rcopy(pc_s.at[lv], pc_r.at[lv, 1], par_s.at[lv, 1], par_r.at[lv, 1], down),
         ]
+
+        def rims(i):
+            for q in range(4):
+                rows = pl.ds(QR * q, QR)
+                wide[cur, i, rows, :] = jnp.where(blk64 == 0, 0.0, roll(wide[cur, 12 + i, rows, :], 1))
+                wide[cur, 18 + i, rows, :] = jnp.where(blk64 == 3, 0.0, roll(wide[cur, 6 + i, rows, :], 3))
+
+        loop(0, 6, rims)
+
+        def local(i):
+            base_lv[...] = dot3(lap[0], lap[1], hl[i, 0], hl[i, 1])
+            for n in range(2):
+                at = i + 6 * n
+                for q in range(4):
+                    rows = pl.ds(QR * q, QR)
+                    value = base_lv[rows, pl.ds(ORB * n, ORB)] + pc_mat[at, rows, :] * wide[cur, 6 + at, rows, :]
+                    for r in range(1, 7):
+                        value = value + HALFW[r] * (wide[cur, 6 + at + r, rows, :] + wide[cur, 6 + at - r, rows, :])
+                    value = scale * value
+                    if lv > 0:
+                        value = value - back * wide[nxt, 6 + at, rows, :]
+                    wide[nxt, 6 + at, rows, :] = value
+
+        loop(0, 6, local)
         for cp in halo_in:
             cp.wait_recv()
 
@@ -323,11 +370,11 @@
             low = HALFW[i + 1] * halo_r[lv, 0, 5]
             for r in range(i + 2, 7):
                 low = low + HALFW[r] * halo_r[lv, 0, 6 + i - r]
-            fix[i] = low
+            fix[i] = scale * low
             high = HALFW[6 - i] * halo_r[lv, 1, 0]
             for r in range(7 - i, 7):
                 high = high + HALFW[r] * halo_r[lv, 1, i + r - 6]
-            fix[6 + i] = high
+            fix[6 + i] = scale * high
         for cp in part_in:
             cp.wait_recv()
         own, dn, hi = pc_s[lv, 0], pc_s[lv, 1], pc_s[lv, 2]
@@ -340,7 +387,7 @@
         corr_high = roll(pc_r[lv, 1, 0], 3) + roll(pc_r[lv, 1, 1], 2) + hi
         beside_low = jnp.where(blk32 == 0, corr_low, roll(corr, 1))
         beside_high = jnp.where(blk32 == 3, corr_high, roll(corr, 3))
-        energy = jnp.concatenate([kbt[...]] * 4, axis=0) * scale
+        energy = jnp.concatenate([kbt] * 4, axis=0) * scale
         for n, value in enumerate((corr, beside_low, beside_high)):
             high, low = split(value * energy)
             high, low = high.astype(F32), low.astype(F32)
@@ -352,65 +399,43 @@
         def finish(i, n, edge):
             ch = jnp.concatenate([cc_h[0], cc_h[n]], axis=0)
             cl = jnp.concatenate([cc_l[0], cc_l[n]], axis=0)
-            base_lv[...] = dot3(cht_h[i], cht_l[i], ch, cl)
+            both = dot(cht_h[i], jnp.concatenate([ch, cl], axis=1))
+            value = both[:, :ORB] + (both[:, ORB:] + dot(cht_l[i], ch))
+            fresh = []
             for q in range(4):
                 rows = pl.ds(QR * q, QR)
                 more = jnp.where(blk64 == edge, roll(fix[i], edge - q), 0.0)
-                wide[nxt, 6 + i, rows, :] = wide[nxt, 6 + i, rows, :] + (base_lv[rows, :] + scale * more)
-
-        loop(0, 6, lambda i: finish(i, 1, 0))
-        loop(6, 12, lambda i: finish(i, 2, 3))
-
-    last = DEGREE % 2
-
-    def pack_out(i):
-        parts = [wide[last, 6 + i, pl.ds(QR * q, QR), :] for q in range(4)]
-        for k, value in enumerate(transpose_blocks(parts)):
-            x_out[k, i] = value
-
-    def first_plane(ch):
-        return (6 * (1 - xh) if ch < 2 else 6 * xh) + 3 * (ch % 2)
-
-    back_in = []
-    back_own = []
-    for ch in range(CH_OUT):
-        first = first_plane(ch)
-        loop(0, 3, lambda i: pack_out(first + i))
-        planes = pl.ds(first, 3)
-        row = []
-        for k in range(1, 4):
-            row.append(
-                rcopy(
-                    x_out.at[(y + k) % 4, planes], r_out.at[y, planes],
-                    out_s.at[k - 1, ch], out_r.at[k - 1, ch], ypeer[k],
-                )
-            )
-        back_in.append(row)
-        own = pltpu.make_async_copy(x_out.at[y, planes], r_out.at[y, planes], loc.at[8 + ch])
-        own.start()
-        back_own.append(own)
+                fresh.append(wide[nxt, 6 + i, rows, :] + (value[QR * q : QR * (q + 1)] + more))
+            if lv == DEGREE - 1:
+                for k, moved in enumerate(transpose_blocks(fresh)):
+                    x_out[k, i] = moved
+            else:
+                packed = jnp.zeros((QR, ORB), F32)
+                for q in range(4):
+                    wide[nxt, 6 + i, pl.ds(QR * q, QR), :] = fresh[q]
+                    packed = jnp.where(blk64 == q, roll(fresh[q], q - edge), packed)
+                halo_s[lv + 1, 1 - edge // 3, i - 2 * edge] = packed
+
+        def finish_two(i, n, edge):
+            finish(i, n, edge)
+            finish(i + 1, n, edge)
+
+        if lv == DEGREE - 1:
+            for ch in range(CH_OUT):
+                n, edge = (1, 0) if ch < 2 else (2, 3)
+                for i in range(3):
+                    finish(3 * ch + i, n, edge)
+                send_out(ch)
+        else:
+            loop(0, 3, lambda i: finish_two(6 + 2 * i, 2, 3))
+            upward = send_halo(lv + 1, 0)
+            loop(0, 3, lambda i: finish_two(2 * i, 1, 0))
+            halo_in = [upward, send_halo(lv + 1, 1)]
 
     def unpack_out(i):
         parts = [r_out[m, i] for m in range(4)]
         for q, value in enumerate(transpose_blocks(parts)):
             filt[i, pl.ds(QR * q, QR), :] = value
-
-    fc_in = []
-    x_recv = []
-    stores = []
-    for ch in range(CH_OUT):
-        first = first_plane(ch)
-        back_own[ch].wait()
-        for cp in back_in[ch]:
-            cp.wait_recv()
-        loop(0, 3, lambda i: unpack_out(first + i))
-        planes = pl.ds(first, 3)
-        if ch < 2:
-            x_recv.append(rcopy(filt.at[planes], xr.at[pl.ds(3 * ch, 3)], xs_s.at[ch], xs_r.at[ch], across))
-        fc_in.append(rcopy(filt.at[planes], filt_c.at[planes], fc_s.at[ch], fc_r.at[ch], core))
-        store = pltpu.make_async_copy(filt.at[planes], out.at[planes], hbm.at[ch])
-        store.start()
-        stores.append(store)
 
     gb[...] = jnp.zeros_like(gb)
 
@@ -423,17 +448,47 @@
         gb[slot] += value[:, :128]
         gb[slot + 1] += value[:, 128:]
 
-    for cp in fc_in:
-        cp.wait_recv()
-    loop(0, CX, lambda i: gram_step(0, filt[i], [filt[i], filt_c[i]]))
+    fc_in = []
+    x_recv = []
+    stores = []
     relay = []
-    for ch in range(2):
+    keep = pl.ds(128 * xh, 128)
+    give = pl.ds(128 * (1 - xh), 128)
+
+    def near(ch):
+        fc_in[ch].wait_recv()
+        loop(3 * ch, 3 * ch + 3, lambda i: gram_step(0, filt[i], [filt[i], filt_c[i]]))
+
+    def pass_on(ch):
         x_recv[ch].wait_recv()
         planes = pl.ds(3 * ch, 3)
         relay.append(rcopy(xr.at[planes], xr2.at[planes], rl_s.at[ch], rl_r.at[ch], core))
-    for ch in range(2):
+
+    def flat_rows(ref, i, rows):
+        return ref[pl.ds(3 * i, 3), rows, :].reshape(3 * 128, ORB)
+
+    for ch in range(CH_OUT):
+        back_own[ch].wait()
+        for cp in back_in[ch]:
+            cp.wait_recv()
+        loop(3 * ch, 3 * ch + 3, unpack_out)
+        planes = pl.ds(3 * ch, 3)
+        x_recv.append(rcopy(filt.at[planes, give], xr.at[planes], xs_s.at[ch], xs_r.at[ch], across))
+        fc_in.append(rcopy(filt.at[planes], filt_c.at[planes], fc_s.at[ch], fc_r.at[ch], core))
+        store = pltpu.make_async_copy(filt.at[planes], out.at[planes], hbm.at[ch])
+        store.start()
+        stores.append(store)
+        if ch > 0:
+            near(ch - 1)
+        if ch > 1:
+            pass_on(ch - 2)
+    near(CH_OUT - 1)
+    every = pl.ds(0, 128)
+    for ch in range(CH_OUT):
+        if ch < 2:
+            pass_on(ch + 2)
         relay[ch].wait_recv()
-        loop(3 * ch, 3 * ch + 3, lambda i: gram_step(2, filt[6 * xh + i], [xr[i], xr2[i]]))
+        gram_step(2, flat_rows(filt, ch, keep), [flat_rows(xr, ch, every), flat_rows(xr2, ch, every)])
     for n in (2, 3):
         gb[n] = jnp.where(xh == 1, gb[n].T, gb[n])
 
@@ -471,10 +526,9 @@
         yg_in.append(rcopy(go.at[y], go.at[y], yg_s.at[k - 1], yg_r.at[k - 1], ypeer[k]))
     for cp in yg_in:
         cp.wait_recv()
-    gram[b] = go[0]
-    gram[core[0]] = go[1]
-    gram[across[0]] = jnp.where(xh == 1, go[2].T, go[2])
-    gram[cross[0]] = jnp.where(xh == 1, go[3].T, go[3])
+    for n, dev in enumerate((b, core[0], across[0], cross[0])):
+        value = go[n] if n < 2 else jnp.where(xh == 1, go[n].T, go[n])
+        gram[:, pl.ds(pl.multiple_of(128 * dev, 128), 128)] = value
 
     pltpu.make_async_copy(sr, sr, ss_s).wait()
     pltpu.make_async_copy(sr, sr, sg_s).wait()
@@ -484,51 +538,51 @@
         cp.wait_send()
 
 
-def run(orb, pot, payload, kbt, lap):
+def run(orb, pot, proj, planes_ref, kb, lap):
     vmem = functools.partial(pltpu.VMEM)
     dma = pltpu.SemaphoreType.DMA
     f = lambda *shape: vmem(shape, F32)
     h = lambda *shape: vmem(shape, BF16)
     scratch = [
+        f(2, 512, 128), f(54, 8, ROWS), f(16, ROWS),
         f(4, CX, QR, ORB), f(4, CX, QR, ORB), f(4, 54, 8, ROWS), f(8, 16, ROWS), f(4, 24, NPROJ, ROWS),
         f(2, 6, NPROJ, ROWS), h(CX, ROWS, ROWS), h(CX, ROWS, ROWS), h(CX, ROWS, ROWS), h(CX, ROWS, ROWS),
-        f(CX, ROWS, ORB), f(2, 24, ROWS, ORB), f(ROWS, ORB),
+        f(CX, ROWS, ORB), f(2, 24, ROWS, ORB), f(ROWS, 2 * ORB), h(6, 2, ROWS, 2 * ORB),
         f(DEGREE, 2, 6, QR, ORB), f(DEGREE, 2, 6, QR, ORB), f(3, 128, ORB),
         f(DEGREE, 3, NPROJ, ORB), f(DEGREE, 2, 3, NPROJ, ORB), h(3, 128, ORB), h(3, 128, ORB), f(CX, QR, ORB),
-        f(4, CX, QR, ORB), f(4, CX, QR, ORB), f(CX, ROWS, ORB), f(CX, ROWS, ORB), f(6, ROWS, ORB), f(6, ROWS, ORB),
+        f(4, CX, QR, ORB), f(4, CX, QR, ORB), f(CX, ROWS, ORB), f(CX, ROWS, ORB), f(CX, 128, ORB), f(CX, 128, ORB),
         f(4, 128, 128), f(3, 128, 128), f(16, 8, 128), f(15, 8, 128), f(8, 128), f(8, 128), f(16, 8, 128),
         f(4, 128, 128),
         dma((3, CH_IN)), dma((3, CH_IN)), dma((3,)), dma((3,)), dma((3,)), dma((3,)), dma((3,)), dma((3,)),
         dma((2,)), dma((2,)), dma((DEGREE, 2)), dma((DEGREE, 2)), dma((DEGREE, 2)), dma((DEGREE, 2)),
-        dma((3, CH_OUT)), dma((3, CH_OUT)), dma((CH_OUT,)), dma((CH_OUT,)), dma((2,)), dma((2,)), dma((2,)), dma((2,)),
+        dma((3, CH_OUT)), dma((3, CH_OUT)), dma((CH_OUT,)), dma((CH_OUT,)),
+        dma((CH_OUT,)), dma((CH_OUT,)), dma((CH_OUT,)), dma((CH_OUT,)),
         dma((3,)), dma((3,)), dma, dma, dma((1,)), dma((1,)), dma, dma, dma((3,)), dma((3,)), dma((16,)), dma((CH_OUT,)),
     ]
     spec = pl.BlockSpec(memory_space=pltpu.VMEM)
+    smem = pl.BlockSpec(memory_space=pltpu.SMEM)
     return pl.pallas_call(
         kernel,
         out_shape=(
             jax.ShapeDtypeStruct((CX, ROWS, ORB), F32),
-            jax.ShapeDtypeStruct((4, 128, 128), F32),
+            jax.ShapeDtypeStruct((128, 512), F32),
         ),
-        in_specs=[spec] * 5,
+        in_specs=[spec, spec, spec, smem, smem, spec],
         out_specs=(pl.BlockSpec(memory_space=pl.ANY), spec),
         scratch_shapes=scratch,
         compiler_params=pltpu.CompilerParams(
             collective_id=0, has_side_effects=True, vmem_limit_bytes=60 * 2**20
         ),
         name="chebyshev",
-    )(orb, pot, payload, kbt, lap)
+    )(orb, pot, proj, planes_ref, kb, lap)
 
 
 def shards(orbitals, potential, projectors, atom_planes, kb_energy):
-    pot = jnp.pad(potential.reshape(CX, ROWS), ((0, 4), (0, 0)))
-    starts = jnp.broadcast_to(
-        atom_planes[:, 0].astype(F32).reshape(2, 1, 2, 1), (2, 8, 2, 128)
-    ).reshape(2, 8, ROWS)
-    payload = jnp.concatenate([projectors.transpose(0, 2, 1, 3).reshape(52, 8, ROWS), starts], axis=0)
-    kbt = jnp.broadcast_to(kb_energy[:, None], (8, ORB))
-    filtered, gram = run(orbitals.reshape(CX, ROWS, ORB), pot, payload, kbt, jnp.asarray(plane_laplacian()))
-    return filtered.reshape(orbitals.shape), gram.transpose(1, 0, 2).reshape(128, 512)
+    filtered, gram = run(
+        orbitals.reshape(CX, ROWS, ORB), potential.reshape(CX, ROWS), projectors, atom_planes, kb_energy,
+        jnp.asarray(plane_laplacian()),
+    )
+    return filtered.reshape(orbitals.shape), gram
 
 
 def solution(mesh):

time: 158 us -> 136 us (0.86)
  Pallas kernels: 146 us -> 128 us
  other arithmetic: 2.59 us -> 0 us
    pallas_call x1, Pallas kernels: 146 us -> 128 us  [run(): pl.pallas_call(kernel, out_shape=(jax.ShapeDtypeStruct((CX, ROWS, ORB), F...]
    concatenate x1 -> x0, other arithmetic: 1.8 us -> none  [shards(): jnp.concatenate([projectors.transpose(0, 2, 1, 3).reshape(52, 8, ROWS), s...]
    unnamed x4 -> x5, local copies, waits for them, and re-layouts: 3.57 us -> 5.35 us
where the time goes in v2:
time: 136 us
  Pallas kernels  128 us (94%)
  local copies, waits for them, and re-layouts  6.94 us (5%)
    pallas_call x1, Pallas kernels, run(): pl.pallas_call(kernel, out_shape=(jax.ShapeDtypeStruct((CX, ROWS, ORB), F...  128 us
    unnamed x5, local copies, waits for them, and re-layouts  5.35 us

profile of v2, /device:TPU:2, one launch (start us, length us, event | category | flops | bytes accessed | tf_op | source)
XLA Modules:
  0.0 136.0 jit_solution(12808512294652160940)
XLA Ops:
  0.6 1.6 %reshape.14.pot = f32[12,256]{1,0:T(8,128)} reshape(f32[12,16,16]{2,1,0:T(8,128)} %param.7) | data formatting | bytes 24576 | tf_op jit(solution)/shard_map/reshape | solution.py:582
  2.2 1.9 %copy.8.proj = f32[4,8,13,256]{3,2,1,0:T(8,128)} copy(f32[4,8,13,256]{3,1,2,0:T(8,128)} %param.8) | data formatting | bytes 851968 | tf_op args[2]
  4.2 128.4 %chebyshev.1 = (f32[12,256,128]{2,1,0:T(8,128)}, f32[128,512]{1,0:T(8,128)}) custom-call(f32[12,256,128]{2,1,0:T(8,128)} %bitcast.2, f32[12,256]{1,0:T(8,128)} %reshape.14.pot, f32[4,8,13,256]{3,2,1,0:T(8,128)} %copy.8.proj, s32[4,13]{1,0:T(4,128)} %planes_ref.1, f32[8]{0:T(128)} %kb.1, bf16[2,256,256]{2,1,0:T(8,128)(2,1)} %constant.2.clone.lap), custom_call_target="tpu_custom_call" | custom-call | tf_op jit(solution)/shard_map/chebyshev/pallas_call | solution.py:564
  132.6 0.0 copy-start
  132.6 2.7 %copy.11 = f32[12,16,16,128]{3,2,1,0:T(8,128)} copy(f32[12,16,16,128]{3,2,1,0:T(8,128)} %bitcast.3) | data formatting | bytes 3145728
  135.3 0.0 copy-done
  135.3 0.7 copy.12
Async XLA Ops:
  132.6 2.7 %copy-start = (f32[128,512]{1,0:T(8,128)S(1)}, f32[128,512]{1,0:T(8,128)}, u32[]{:S(2)}) copy-start(f32[128,512]{1,0:T(8,128)} %get-tuple-element.9) | copy-start | bytes 786436

commit v3 on v2

--- a/solution.py
+++ b/solution.py
@@ -17,7 +17,8 @@
 NPROJ = 32
 CELLS = 196608
 CH_IN = 3
-CH_OUT = 4
+CH_OUT = 6
+PART_OUT = CX // CH_OUT
 WEIGHTS = (
     -5369.0 / 1800.0,
     12.0 / 7.0,
@@ -70,6 +71,13 @@
     return high, (value - high.astype(F32)).astype(BF16)
 
 
+def split3(value):
+    high = value.astype(BF16)
+    rest = value - high.astype(F32)
+    mid = rest.astype(BF16)
+    return high, mid, (rest - mid.astype(F32)).astype(BF16)
+
+
 def dot(a, b):
     return jnp.dot(a, b, preferred_element_type=F32)
 
@@ -114,24 +122,27 @@
 
 def kernel(
     orb, pot, proj, planes_ref, kb, lap, out, gram,
-    flat, payload, pot_s16, x_in, r_in, pg, potg, cm, rim, chi_h, chi_l, cht_h, cht_l, pc_mat, wide, base_lv, hl,
+    payload, pot_s16, x_in, r_in, pg, potg, cm, rim, chi_h, chi_l, cht_h, cht_l, pc_mat, wide, base_lv, hl,
     halo_s, halo_r, part, pc_s, pc_r, cc_h, cc_l, fix,
-    x_out, r_out, filt, filt_c, xr, xr2, gb, yr, sb, sr, st, xt, tb, go,
-    in_s, in_r, chi_s, chi_r, cor_s, cor_r, pot_s, pot_r, rim_s, rim_r, hal_s, hal_r, par_s, par_r,
-    out_s, out_r, fc_s, fc_r, xs_s, xs_r, rl_s, rl_r, ys_s, ys_r, ss_s, ss_r, xh_s, xh_r, sg_s, sg_r, yg_s, yg_r, loc, hbm,
+    x_out, r_out, filt, filt_c, xr, xr2, gb, z_r, zs, y_r, ws, x1_r, x2_r, go,
+    in_s, in_r, chi_s, chi_r, acr_s, acr_r, cor_s, cor_r, pot_s, pot_r, rim_s, rim_r, hal_s, hal_r, par_s, par_r,
+    out_s, out_r, fc_s, fc_r, xs_s, xs_r, rl_s, rl_r, za_s, za_r, zb_s, zb_r, ye_s, ye_r, xe_s, xe_r, zg_s, zg_r, loc, hbm,
 ):
     middle, scales, recall = filter_terms(DEGREE)
     b = lax.axis_index("band")
     g = lax.axis_index("grid")
     s, y = g // 4, g % 4
+    z, xl = s % 8, s // 8
     xh, c = b // 2, b % 2
     core = (2 * xh + 1 - c, g)
     across = (2 * (1 - xh) + c, g)
     cross = (2 * (1 - xh) + 1 - c, g)
+    other = (g + 32) % 64
     up = (b, (g + 4) % 64)
     down = (b, (g + 60) % 64)
     ypeer = [None] + [(b, 4 * s + (y + k) % 4) for k in range(1, 4)]
-    speer = [None] + [(b, (g + 4 * d) % 64) for d in range(1, 16)]
+    zpeer = [None] + [(b, 32 * xl + 4 * ((z + k) % 8) + y) for k in range(1, 8)]
+    xpeers = [(b, other), across, (across[0], other), cross, (cross[0], other)]
     pending = []
 
     def rcopy(src, dst, ssem, rsem, dev):
@@ -143,32 +154,38 @@
         return cp
 
     barrier = pltpu.get_barrier_semaphore()
-    friends = ypeer[1:] + speer[1:] + [core, across, cross]
+    friends = ypeer[1:] + zpeer[1:] + xpeers + [up, down, core]
     for dev in friends:
         pl.semaphore_signal(barrier, inc=1, device_id=dev, device_id_type=MESH)
 
+    payload[pl.ds(0, 52)] = proj[...]
+    payload[pl.ds(54, 2)] = jnp.zeros((2, 8, ROWS), F32)
     for j in range(4):
-        for p in range(8):
-            for lh in range(2):
-                flat[lh, pl.ds(128 * j + 16 * p, 13), :] = proj[j, p, :, pl.ds(128 * lh, 128)]
-    for j in range(4):
-        for n in range(13):
-            for lh in range(2):
-                payload[13 * j + n, :, pl.ds(128 * lh, 128)] = flat[lh, pl.ds(128 * j + n, 8, stride=16), :]
         payload[52 + j // 2, :, pl.ds(128 * (j % 2), 128)] = jnp.full((8, 128), planes_ref[j, 0].astype(F32))
-    pot_s16[pl.ds(0, 8), :] = pot[pl.ds(0, 8), :]
-    pot_s16[pl.ds(8, 8), :] = jnp.concatenate([pot[pl.ds(8, 4), :], jnp.zeros((4, ROWS), F32)], axis=0)
+    p_pick = (
+        lax.broadcasted_iota(jnp.int32, (16, ROWS), 1) % 16 == lax.broadcasted_iota(jnp.int32, (16, ROWS), 0)
+    )
+    p_pick = jnp.where(p_pick, 1.0, 0.0).astype(BF16)
+    p_high, p_mid, p_low = split3(pot[...].reshape(16 * CX, 16))
+    wide_pot = dot(p_high, p_pick) + (dot(p_mid, p_pick) + dot(p_low, p_pick))
+    p_mine = (
+        lax.broadcasted_iota(jnp.int32, (16 * CX, ROWS), 1) // 16
+        == lax.broadcasted_iota(jnp.int32, (16 * CX, ROWS), 0) % 16
+    )
+    rows_pot = jnp.sum(jnp.where(p_mine, wide_pot, 0.0).reshape(CX, 16, ROWS), axis=1)
+    pot_s16[...] = jnp.concatenate([rows_pot, jnp.zeros((4, ROWS), F32)], axis=0)
     p_row = lax.broadcasted_iota(jnp.int32, (8, ORB), 0)
     kbt = jnp.zeros((8, ORB), F32)
     for p in range(8):
         kbt = jnp.where(p_row == p, kb[p], kbt)
     pl.semaphore_wait(barrier, len(friends))
 
-    half = pl.ds(27 * c, 27)
+    mine = pl.ds(14 * b, 14)
+    theirs = pl.ds(14 * across[0], 14)
     chi_in = [None]
     pot_in = [None]
     for k in range(1, 4):
-        chi_in.append(rcopy(payload.at[half], pg.at[y, half], chi_s.at[k - 1], chi_r.at[k - 1], ypeer[k]))
+        chi_in.append(rcopy(payload.at[mine], pg.at[y, mine], chi_s.at[k - 1], chi_r.at[k - 1], ypeer[k]))
         pot_in.append(rcopy(pot_s16, potg.at[y], pot_s.at[k - 1], pot_r.at[k - 1], ypeer[k]))
     own_pg = pltpu.make_async_copy(payload, pg.at[y], loc.at[0])
     own_pg.start()
@@ -206,10 +223,7 @@
     for k in range(1, 4):
         pot_in[k].wait_recv()
     pot_t = potg[...].reshape(128, ROWS).T
-    p_high = pot_t.astype(BF16)
-    rest = pot_t - p_high.astype(F32)
-    p_mid = rest.astype(BF16)
-    p_low = (rest - p_mid.astype(F32)).astype(BF16)
+    p_high, p_mid, p_low = split3(pot_t)
     centre = 3.0 * HALFW[0] - middle
     e_row = lax.broadcasted_iota(jnp.int32, (128, ORB), 0)
     e_same = (e_row // 16) == lane_block(128)
@@ -220,14 +234,20 @@
 
     loop(0, CX, spread_pot)
 
-    cor_in = [None]
+    acr_in = []
+    cor_in = []
     own_pg.wait()
     for k in range(1, 4):
         chi_in[k].wait_recv()
         src = (y + 4 - k) % 4
-        cor_in.append(rcopy(pg.at[src, half], pg.at[src, half], cor_s.at[k - 1], cor_r.at[k - 1], core))
+        acr_in.append(rcopy(pg.at[src, mine], pg.at[src, mine], acr_s.at[k - 1], acr_r.at[k - 1], across))
+        cor_in.append(rcopy(pg.at[src, mine], pg.at[src, mine], cor_s.at[0, k - 1], cor_r.at[0, k - 1], core))
     for k in range(1, 4):
-        cor_in[k].wait_recv()
+        acr_in[k - 1].wait_recv()
+        src = (y + 4 - k) % 4
+        cor_in.append(rcopy(pg.at[src, theirs], pg.at[src, theirs], cor_s.at[1, k - 1], cor_r.at[1, k - 1], core))
+    for cp in cor_in:
+        cp.wait_recv()
 
     def place(dom):
         for j in range(4):
@@ -253,16 +273,14 @@
         rcopy(cm.at[3, pl.ds(18, 6)], rim.at[0], rim_s.at[0], rim_r.at[0], up),
         rcopy(cm.at[0, pl.ds(0, 6)], rim.at[1], rim_s.at[1], rim_r.at[1], down),
     ]
-    for cp in rim_in:
-        cp.wait_recv()
-
-    def make_chi(i, beside):
-        mat = jnp.concatenate([cm[d, i + 6] for d in range(4)] + beside, axis=0)
-        chi_h[i], chi_l[i] = split(mat)
-        cht_h[i], cht_l[i] = split(mat.T)
-
-    loop(0, 6, lambda i: make_chi(i, [rim[0, i]] + [cm[d, i + 18] for d in range(3)]))
-    loop(6, 12, lambda i: make_chi(i, [cm[d, i - 6] for d in range(1, 4)] + [rim[1, i - 6]]))
+
+    def make_chi(i, first, blocks):
+        mat = jnp.concatenate(blocks, axis=0)
+        rows = pl.ds(first, 128)
+        chi_h[i, rows, :], chi_l[i, rows, :] = split(mat)
+        cht_h[i, :, rows], cht_l[i, :, rows] = split(mat.T)
+
+    loop(0, CX, lambda i: make_chi(i, 0, [cm[d, i + 6] for d in range(4)]))
 
     def unpack_in(i):
         parts = [r_in[m, i] for m in range(4)]
@@ -297,7 +315,7 @@
     back_own = []
 
     def send_out(ch):
-        planes = pl.ds(3 * ch, 3)
+        planes = pl.ds(PART_OUT * ch, PART_OUT)
         row = []
         for k in range(1, 4):
             row.append(
@@ -313,6 +331,10 @@
 
     loop(0, 6, pack_halo)
     halo_in = [send_halo(0, 0), send_halo(0, 1)]
+    for cp in rim_in:
+        cp.wait_recv()
+    loop(0, 6, lambda i: make_chi(i, 128, [rim[0, i]] + [cm[d, i + 18] for d in range(3)]))
+    loop(6, 12, lambda i: make_chi(i, 128, [cm[d, i - 6] for d in range(1, 4)] + [rim[1, i - 6]]))
     for lv in range(DEGREE):
         cur, nxt = lv % 2, 1 - lv % 2
         scale, back = scales[lv], recall[lv]
@@ -422,9 +444,9 @@
 
         if lv == DEGREE - 1:
             for ch in range(CH_OUT):
-                n, edge = (1, 0) if ch < 2 else (2, 3)
-                for i in range(3):
-                    finish(3 * ch + i, n, edge)
+                n, edge = (1, 0) if 2 * ch < CH_OUT else (2, 3)
+                for i in range(PART_OUT):
+                    finish(PART_OUT * ch + i, n, edge)
                 send_out(ch)
         else:
             loop(0, 3, lambda i: finish_two(6 + 2 * i, 2, 3))
@@ -457,22 +479,22 @@
 
     def near(ch):
         fc_in[ch].wait_recv()
-        loop(3 * ch, 3 * ch + 3, lambda i: gram_step(0, filt[i], [filt[i], filt_c[i]]))
+        loop(PART_OUT * ch, PART_OUT * (ch + 1), lambda i: gram_step(0, filt[i], [filt[i], filt_c[i]]))
 
     def pass_on(ch):
         x_recv[ch].wait_recv()
-        planes = pl.ds(3 * ch, 3)
+        planes = pl.ds(PART_OUT * ch, PART_OUT)
         relay.append(rcopy(xr.at[planes], xr2.at[planes], rl_s.at[ch], rl_r.at[ch], core))
 
     def flat_rows(ref, i, rows):
-        return ref[pl.ds(3 * i, 3), rows, :].reshape(3 * 128, ORB)
+        return ref[pl.ds(PART_OUT * i, PART_OUT), rows, :].reshape(PART_OUT * 128, ORB)
 
     for ch in range(CH_OUT):
         back_own[ch].wait()
         for cp in back_in[ch]:
             cp.wait_recv()
-        loop(3 * ch, 3 * ch + 3, unpack_out)
-        planes = pl.ds(3 * ch, 3)
+        loop(PART_OUT * ch, PART_OUT * (ch + 1), unpack_out)
+        planes = pl.ds(PART_OUT * ch, PART_OUT)
         x_recv.append(rcopy(filt.at[planes, give], xr.at[planes], xs_s.at[ch], xs_r.at[ch], across))
         fc_in.append(rcopy(filt.at[planes], filt_c.at[planes], fc_s.at[ch], fc_r.at[ch], core))
         store = pltpu.make_async_copy(filt.at[planes], out.at[planes], hbm.at[ch])
@@ -480,58 +502,62 @@
         stores.append(store)
         if ch > 0:
             near(ch - 1)
-        if ch > 1:
-            pass_on(ch - 2)
+        if ch > 2:
+            pass_on(ch - 3)
     near(CH_OUT - 1)
+
+    def to_z(first, ssem, rsem):
+        for k in range(1, 8):
+            pltpu.make_async_remote_copy(
+                src_ref=gb.at[pl.ds(first, 2), pl.ds(16 * ((z + k) % 8), 16)], dst_ref=z_r.at[first // 2, k - 1],
+                send_sem=ssem, recv_sem=rsem, device_id=zpeer[k], device_id_type=MESH,
+            ).start()
+
     every = pl.ds(0, 128)
     for ch in range(CH_OUT):
-        if ch < 2:
-            pass_on(ch + 2)
+        if ch + 3 < CH_OUT:
+            pass_on(ch + 3)
+        if ch == 0:
+            to_z(0, za_s, za_r)
         relay[ch].wait_recv()
         gram_step(2, flat_rows(filt, ch, keep), [flat_rows(xr, ch, every), flat_rows(xr2, ch, every)])
     for n in (2, 3):
         gb[n] = jnp.where(xh == 1, gb[n].T, gb[n])
 
-    y_in = []
-    for k in range(1, 4):
-        y_in.append(rcopy(gb.at[(y + k) % 4], yr.at[k - 1], ys_s.at[k - 1], ys_r.at[k - 1], ypeer[k]))
+    to_z(2, zb_s, zb_r)
+    tile = pl.ds(16 * z, 16)
+    for n, sem in ((0, za_r), (1, zb_r)):
+        pltpu.make_async_copy(z_r.at[n], z_r.at[n], sem).wait()
+        value = gb[pl.ds(2 * n, 2), tile, :]
+        for k in range(7):
+            value = value + z_r[n, k]
+        zs[pl.ds(2 * n, 2)] = value
+    y_in = [rcopy(zs, y_r.at[k - 1], ye_s.at[k - 1], ye_r.at[k - 1], ypeer[k]) for k in range(1, 4)]
     for cp in y_in:
         cp.wait_recv()
-    sb[...] = (gb[y] + (yr[0] + (yr[1] + yr[2]))).reshape(16, 8, 128)
-    for d in range(1, 16):
-        cp = pltpu.make_async_remote_copy(
-            src_ref=sb.at[(s + d) % 16], dst_ref=sr.at[d - 1], send_sem=ss_s, recv_sem=ss_r,
-            device_id=speer[d], device_id_type=MESH,
-        )
-        cp.start()
-    pltpu.make_async_copy(sr, sr, ss_r).wait()
-    tile = sb[s]
-    for d in range(15):
-        tile = tile + sr[d]
-    st[...] = tile
-    partner = (2 * (1 - xh) + (c + y // 3 * (1 - 2 * c)), g)
-    xh_in = rcopy(st, xt, xh_s.at[0], xh_r.at[0], partner)
-    xh_in.wait_recv()
-    tb[s] = tile + jnp.where(y >= 2, xt[...], 0.0)
-    for d in range(1, 16):
-        cp = pltpu.make_async_remote_copy(
-            src_ref=tb.at[s], dst_ref=tb.at[s], send_sem=sg_s, recv_sem=sg_r,
-            device_id=speer[d], device_id_type=MESH,
-        )
-        cp.start()
-    pltpu.make_async_copy(sr, sr, sg_r).wait()
-    go[y] = tb[...].reshape(128, 128) * (1.0 / CELLS)
-    yg_in = []
-    for k in range(1, 4):
-        yg_in.append(rcopy(go.at[y], go.at[y], yg_s.at[k - 1], yg_r.at[k - 1], ypeer[k]))
-    for cp in yg_in:
+    ws[...] = zs[...] + (y_r[0] + (y_r[1] + y_r[2]))
+    x_in2 = [rcopy(ws, x1_r, xe_s.at[0], xe_r.at[0], xpeers[0])]
+    for k in range(1, 5):
+        x_in2.append(rcopy(ws.at[2 + (k - 1) // 2], x2_r.at[k - 1], xe_s.at[k], xe_r.at[k], xpeers[k]))
+    for cp in x_in2:
         cp.wait_recv()
+    pair = ws[...] + x1_r[...]
+    go[pl.ds(0, 2), tile, :] = pair[:2] * (1.0 / CELLS)
+    go[2, tile, :] = (pair[2] + (x2_r[0] + x2_r[1])) * (1.0 / CELLS)
+    go[3, tile, :] = (pair[3] + (x2_r[2] + x2_r[3])) * (1.0 / CELLS)
+    for k in range(1, 8):
+        pltpu.make_async_remote_copy(
+            src_ref=go.at[:, tile], dst_ref=go.at[:, tile], send_sem=zg_s, recv_sem=zg_r,
+            device_id=zpeer[k], device_id_type=MESH,
+        ).start()
+    pltpu.make_async_copy(z_r, z_r, zg_r).wait()
     for n, dev in enumerate((b, core[0], across[0], cross[0])):
         value = go[n] if n < 2 else jnp.where(xh == 1, go[n].T, go[n])
         gram[:, pl.ds(pl.multiple_of(128 * dev, 128), 128)] = value
 
-    pltpu.make_async_copy(sr, sr, ss_s).wait()
-    pltpu.make_async_copy(sr, sr, sg_s).wait()
+    pltpu.make_async_copy(z_r.at[0], z_r.at[0], za_s).wait()
+    pltpu.make_async_copy(z_r.at[1], z_r.at[1], zb_s).wait()
+    pltpu.make_async_copy(z_r, z_r, zg_s).wait()
     for cp in stores:
         cp.wait()
     for cp in pending:
@@ -544,20 +570,21 @@
     f = lambda *shape: vmem(shape, F32)
     h = lambda *shape: vmem(shape, BF16)
     scratch = [
-        f(2, 512, 128), f(54, 8, ROWS), f(16, ROWS),
-        f(4, CX, QR, ORB), f(4, CX, QR, ORB), f(4, 54, 8, ROWS), f(8, 16, ROWS), f(4, 24, NPROJ, ROWS),
+        f(56, 8, ROWS), f(16, ROWS),
+        f(4, CX, QR, ORB), f(4, CX, QR, ORB), f(4, 56, 8, ROWS), f(8, 16, ROWS), f(4, 24, NPROJ, ROWS),
         f(2, 6, NPROJ, ROWS), h(CX, ROWS, ROWS), h(CX, ROWS, ROWS), h(CX, ROWS, ROWS), h(CX, ROWS, ROWS),
         f(CX, ROWS, ORB), f(2, 24, ROWS, ORB), f(ROWS, 2 * ORB), h(6, 2, ROWS, 2 * ORB),
         f(DEGREE, 2, 6, QR, ORB), f(DEGREE, 2, 6, QR, ORB), f(3, 128, ORB),
         f(DEGREE, 3, NPROJ, ORB), f(DEGREE, 2, 3, NPROJ, ORB), h(3, 128, ORB), h(3, 128, ORB), f(CX, QR, ORB),
         f(4, CX, QR, ORB), f(4, CX, QR, ORB), f(CX, ROWS, ORB), f(CX, ROWS, ORB), f(CX, 128, ORB), f(CX, 128, ORB),
-        f(4, 128, 128), f(3, 128, 128), f(16, 8, 128), f(15, 8, 128), f(8, 128), f(8, 128), f(16, 8, 128),
-        f(4, 128, 128),
-        dma((3, CH_IN)), dma((3, CH_IN)), dma((3,)), dma((3,)), dma((3,)), dma((3,)), dma((3,)), dma((3,)),
+        f(4, 128, 128), f(2, 7, 2, 16, 128), f(4, 16, 128), f(3, 4, 16, 128), f(4, 16, 128), f(4, 16, 128),
+        f(4, 16, 128), f(4, 128, 128),
+        dma((3, CH_IN)), dma((3, CH_IN)), dma((3,)), dma((3,)), dma((3,)), dma((3,)), dma((2, 3)), dma((2, 3)),
+        dma((3,)), dma((3,)),
         dma((2,)), dma((2,)), dma((DEGREE, 2)), dma((DEGREE, 2)), dma((DEGREE, 2)), dma((DEGREE, 2)),
         dma((3, CH_OUT)), dma((3, CH_OUT)), dma((CH_OUT,)), dma((CH_OUT,)),
         dma((CH_OUT,)), dma((CH_OUT,)), dma((CH_OUT,)), dma((CH_OUT,)),
-        dma((3,)), dma((3,)), dma, dma, dma((1,)), dma((1,)), dma, dma, dma((3,)), dma((3,)), dma((16,)), dma((CH_OUT,)),
+        dma, dma, dma, dma, dma((3,)), dma((3,)), dma((5,)), dma((5,)), dma, dma, dma((16,)), dma((CH_OUT,)),
     ]
     spec = pl.BlockSpec(memory_space=pltpu.VMEM)
     smem = pl.BlockSpec(memory_space=pltpu.SMEM)
@@ -579,7 +606,8 @@
 
 def shards(orbitals, potential, projectors, atom_planes, kb_energy):
     filtered, gram = run(
-        orbitals.reshape(CX, ROWS, ORB), potential.reshape(CX, ROWS), projectors, atom_planes, kb_energy,
+        orbitals.reshape(CX, ROWS, ORB), potential, projectors.transpose(0, 2, 1, 3).reshape(52, 8, ROWS),
+        atom_planes, kb_energy,
         jnp.asarray(plane_laplacian()),
     )
     return filtered.reshape(orbitals.shape), gram

time: 136 us -> 129 us (0.949)
  Pallas kernels: 128 us -> 124 us
  local copies, waits for them, and re-layouts: 6.94 us -> 3.4 us
    pallas_call x1, Pallas kernels: 128 us -> 124 us  [run(): pl.pallas_call(kernel, out_shape=(jax.ShapeDtypeStruct((CX, ROWS, ORB), F...]
    unnamed x5 -> x4, local copies, waits for them, and re-layouts: 5.35 us -> 3.4 us
    reshape x1 -> x0, local copies, waits for them, and re-layouts: 1.59 us -> none  [shards(): potential.reshape(CX, ROWS)]
where the time goes in v3:
time: 129 us; the launch traced here: 128 us
  Pallas kernels  124 us (96%)
  local copies, waits for them, and re-layouts  3.4 us (3%)
    pallas_call x1, Pallas kernels, run(): pl.pallas_call(kernel, out_shape=(jax.ShapeDtypeStruct((CX, ROWS, ORB), F...  124 us
    unnamed x4, local copies, waits for them, and re-layouts  3.4 us

profile of v3, /device:TPU:2, one launch (start us, length us, event | category | flops | bytes accessed | tf_op | source)
XLA Modules:
  0.0 128.1 jit_solution(7221667448456941433)
XLA Ops:
  0.6 124.0 %chebyshev.1 = (f32[12,256,128]{2,1,0:T(8,128)}, f32[128,512]{1,0:T(8,128)}) custom-call(f32[12,256,128]{2,1,0:T(8,128)} %bitcast.5, f32[12,16,16]{2,1,0:T(8,128)} %pot.1, f32[52,8,256]{2,1,0:T(8,128)} %bitcast.7, s32[4,13]{1,0:T(4,128)} %planes_ref.1, f32[8]{0:T(128)} %kb.1, bf16[2,256,256]{2,1,0:T(8,128)(2,1)} %constant.2.clone.lap), custom_call_target="tpu_custom_call" | custom-call | tf_op jit(solution)/shard_map/chebyshev/pallas_call | solution.py:591
  124.7 0.0 copy-start
  124.7 2.7 %copy.10 = f32[12,16,16,128]{3,2,1,0:T(8,128)} copy(f32[12,16,16,128]{3,2,1,0:T(8,128)} %bitcast.6) | data formatting | bytes 3145728
  127.4 0.0 copy-done
  127.4 0.7 copy.11
Async XLA Ops:
  124.7 2.7 %copy-start = (f32[128,512]{1,0:T(8,128)S(1)}, f32[128,512]{1,0:T(8,128)}, u32[]{:S(2)}) copy-start(f32[128,512]{1,0:T(8,128)} %get-tuple-element.9) | copy-start | bytes 786436

commit v4 on v3

--- a/solution.py
+++ b/solution.py
@@ -116,8 +116,8 @@
     )
 
 
-def loop(start, stop, body):
-    lax.fori_loop(start, stop, lambda i, c: (body(i), c)[1], 0)
+def loop(start, stop, body, unroll=1):
+    lax.fori_loop(start, stop, lambda i, c: (body(i), c)[1], 0, unroll=unroll)
 
 
 def kernel(
@@ -178,6 +178,12 @@
     kbt = jnp.zeros((8, ORB), F32)
     for p in range(8):
         kbt = jnp.where(p_row == p, kb[p], kbt)
+    def pack_in(i):
+        parts = [orb[i, pl.ds(QR * q, QR), :] for q in range(4)]
+        for k, value in enumerate(transpose_blocks(parts)):
+            x_in[k, i] = value
+
+    loop(0, CX, pack_in, 2)
     pl.semaphore_wait(barrier, len(friends))
 
     mine = pl.ds(14 * b, 14)
@@ -196,13 +202,7 @@
     orb_in = []
     orb_own = []
 
-    def pack_in(i):
-        parts = [orb[i, pl.ds(QR * q, QR), :] for q in range(4)]
-        for k, value in enumerate(transpose_blocks(parts)):
-            x_in[k, i] = value
-
     for ch in range(CH_IN):
-        loop(span * ch, span * (ch + 1), pack_in)
         planes = pl.ds(span * ch, span)
         row = []
         for k in range(1, 4):
@@ -217,6 +217,14 @@
         own.start()
         orb_own.append(own)
 
+    acr_in = []
+    cor_in = []
+    own_pg.wait()
+    for k in range(1, 4):
+        chi_in[k].wait_recv()
+        src = (y + 4 - k) % 4
+        acr_in.append(rcopy(pg.at[src, mine], pg.at[src, mine], acr_s.at[k - 1], acr_r.at[k - 1], across))
+        cor_in.append(rcopy(pg.at[src, mine], pg.at[src, mine], cor_s.at[0, k - 1], cor_r.at[0, k - 1], core))
     for slot in range(4, 8):
         potg[slot] = jnp.zeros((16, ROWS), F32)
     own_pot.wait()
@@ -234,14 +242,6 @@
 
     loop(0, CX, spread_pot)
 
-    acr_in = []
-    cor_in = []
-    own_pg.wait()
-    for k in range(1, 4):
-        chi_in[k].wait_recv()
-        src = (y + 4 - k) % 4
-        acr_in.append(rcopy(pg.at[src, mine], pg.at[src, mine], acr_s.at[k - 1], acr_r.at[k - 1], across))
-        cor_in.append(rcopy(pg.at[src, mine], pg.at[src, mine], cor_s.at[0, k - 1], cor_r.at[0, k - 1], core))
     for k in range(1, 4):
         acr_in[k - 1].wait_recv()
         src = (y + 4 - k) % 4
@@ -282,6 +282,11 @@
 
     loop(0, CX, lambda i: make_chi(i, 0, [cm[d, i + 6] for d in range(4)]))
 
+    for cp in rim_in:
+        cp.wait_recv()
+    loop(0, 6, lambda i: make_chi(i, 128, [rim[0, i]] + [cm[d, i + 18] for d in range(3)]))
+    loop(6, 12, lambda i: make_chi(i, 128, [cm[d, i - 6] for d in range(1, 4)] + [rim[1, i - 6]]))
+
     def unpack_in(i):
         parts = [r_in[m, i] for m in range(4)]
         for q, value in enumerate(transpose_blocks(parts)):
@@ -297,9 +302,11 @@
     blk64 = lane_block(QR)
     blk32 = lane_block(NPROJ)
 
-    def send_halo(lv, side):
+    def send_halo(lv, side, piece):
+        planes = (pl.ds(0, 2), pl.ds(2, 4))[piece]
         return rcopy(
-            halo_s.at[lv, side], halo_r.at[lv, side], hal_s.at[lv, side], hal_r.at[lv, side], (up, down)[side]
+            halo_s.at[lv, side, planes], halo_r.at[lv, side, planes],
+            hal_s.at[lv, side, piece], hal_r.at[lv, side, piece], (up, down)[side],
         )
 
     def pack_halo(i):
@@ -330,11 +337,15 @@
         back_own.append(own)
 
     loop(0, 6, pack_halo)
-    halo_in = [send_halo(0, 0), send_halo(0, 1)]
-    for cp in rim_in:
-        cp.wait_recv()
-    loop(0, 6, lambda i: make_chi(i, 128, [rim[0, i]] + [cm[d, i + 18] for d in range(3)]))
-    loop(6, 12, lambda i: make_chi(i, 128, [cm[d, i - 6] for d in range(1, 4)] + [rim[1, i - 6]]))
+    halo_in = [send_halo(0, 0, 0), send_halo(0, 1, 0)]
+
+    def mended(buf, i, edge):
+        groups = []
+        for q in range(4):
+            more = jnp.where(blk64 == edge, roll(fix[i], edge - q), 0.0)
+            groups.append(wide[buf, 6 + i, pl.ds(QR * q, QR), :] + more)
+        return groups
+
     for lv in range(DEGREE):
         cur, nxt = lv % 2, 1 - lv % 2
         scale, back = scales[lv], recall[lv]
@@ -343,7 +354,12 @@
         def partials(i):
             for n in range(2):
                 at = i + 6 * n
-                high, low = split(wide[cur, 6 + at])
+                if lv == 0:
+                    value = wide[cur, 6 + at]
+                else:
+                    value = jnp.concatenate(mended(cur, at, 3 * n), axis=0)
+                    wide[cur, 6 + at] = value
+                high, low = split(value)
                 hl[i, 0, :, pl.ds(ORB * n, ORB)] = high
                 hl[i, 1, :, pl.ds(ORB * n, ORB)] = low
                 both = dot(chi_h[at], jnp.concatenate([high, low], axis=1))
@@ -351,16 +367,20 @@
                 part[0] += value[:128]
                 part[1 + n] += value[128:]
 
-        loop(0, 6, partials)
+        loop(0, 6, partials, 6)
         for n in range(3):
             packed = jnp.zeros((NPROJ, ORB), F32)
             for d in range(4):
                 packed = jnp.where(blk32 == d, part[n, pl.ds(NPROJ * d, NPROJ), :], packed)
             pc_s[lv, n] = packed
+        own, dn, hi = pc_s[lv, 0], pc_s[lv, 1], pc_s[lv, 2]
+        pc_s[lv, 3] = roll(hi, 2) + jnp.where(blk32 == 0, roll(own, 1), 0.0)
+        pc_s[lv, 4] = roll(dn, 2) + jnp.where(blk32 == 3, roll(own, 3), 0.0)
         part_in = [
-            rcopy(pc_s.at[lv], pc_r.at[lv, 0], par_s.at[lv, 0], par_r.at[lv, 0], up),
-            rcopy(pc_s.at[lv], pc_r.at[lv, 1], par_s.at[lv, 1], par_r.at[lv, 1], down),
+            rcopy(pc_s.at[lv, 3], pc_r.at[lv, 0], par_s.at[lv, 0], par_r.at[lv, 0], up),
+            rcopy(pc_s.at[lv, 4], pc_r.at[lv, 1], par_s.at[lv, 1], par_r.at[lv, 1], down),
         ]
+        halo_rest = [send_halo(lv, 0, 1), send_halo(lv, 1, 1)]
 
         def rims(i):
             for q in range(4):
@@ -384,29 +404,18 @@
                         value = value - back * wide[nxt, 6 + at, rows, :]
                     wide[nxt, 6 + at, rows, :] = value
 
-        loop(0, 6, local)
-        for cp in halo_in:
-            cp.wait_recv()
-
-        for i in range(6):
-            low = HALFW[i + 1] * halo_r[lv, 0, 5]
-            for r in range(i + 2, 7):
-                low = low + HALFW[r] * halo_r[lv, 0, 6 + i - r]
-            fix[i] = scale * low
-            high = HALFW[6 - i] * halo_r[lv, 1, 0]
-            for r in range(7 - i, 7):
-                high = high + HALFW[r] * halo_r[lv, 1, i + r - 6]
-            fix[6 + i] = scale * high
+        loop(0, 6, local, 6)
         for cp in part_in:
             cp.wait_recv()
         own, dn, hi = pc_s[lv, 0], pc_s[lv, 1], pc_s[lv, 2]
+        below, above = pc_r[lv, 0], pc_r[lv, 1]
         corr = (
             own
-            + jnp.where(blk32 == 0, roll(pc_r[lv, 0, 2], 1), roll(hi, 1))
-            + jnp.where(blk32 == 3, roll(pc_r[lv, 1, 1], 3), roll(dn, 3))
+            + jnp.where(blk32 == 0, roll(below, 3), roll(hi, 1))
+            + jnp.where(blk32 == 3, roll(above, 1), roll(dn, 3))
         )
-        corr_low = roll(pc_r[lv, 0, 0], 1) + roll(pc_r[lv, 0, 2], 2) + dn
-        corr_high = roll(pc_r[lv, 1, 0], 3) + roll(pc_r[lv, 1, 1], 2) + hi
+        corr_low = below + dn
+        corr_high = above + hi
         beside_low = jnp.where(blk32 == 0, corr_low, roll(corr, 1))
         beside_high = jnp.where(blk32 == 3, corr_high, roll(corr, 3))
         energy = jnp.concatenate([kbt] * 4, axis=0) * scale
@@ -418,41 +427,56 @@
                 cc_h[n, rows, :] = jnp.where(blk32 == d, high, 0.0).astype(BF16)
                 cc_l[n, rows, :] = jnp.where(blk32 == d, low, 0.0).astype(BF16)
 
-        def finish(i, n, edge):
+        def spread(i, n, edge):
             ch = jnp.concatenate([cc_h[0], cc_h[n]], axis=0)
             cl = jnp.concatenate([cc_l[0], cc_l[n]], axis=0)
             both = dot(cht_h[i], jnp.concatenate([ch, cl], axis=1))
             value = both[:, :ORB] + (both[:, ORB:] + dot(cht_l[i], ch))
-            fresh = []
+            packed = jnp.zeros((QR, ORB), F32)
             for q in range(4):
                 rows = pl.ds(QR * q, QR)
-                more = jnp.where(blk64 == edge, roll(fix[i], edge - q), 0.0)
-                fresh.append(wide[nxt, 6 + i, rows, :] + (value[QR * q : QR * (q + 1)] + more))
-            if lv == DEGREE - 1:
-                for k, moved in enumerate(transpose_blocks(fresh)):
-                    x_out[k, i] = moved
-            else:
-                packed = jnp.zeros((QR, ORB), F32)
-                for q in range(4):
-                    wide[nxt, 6 + i, pl.ds(QR * q, QR), :] = fresh[q]
-                    packed = jnp.where(blk64 == q, roll(fresh[q], q - edge), packed)
+                fresh = wide[nxt, 6 + i, rows, :] + value[QR * q : QR * (q + 1)]
+                wide[nxt, 6 + i, rows, :] = fresh
+                packed = jnp.where(blk64 == q, roll(fresh, q - edge), packed)
+            if lv + 1 < DEGREE:
                 halo_s[lv + 1, 1 - edge // 3, i - 2 * edge] = packed
 
-        def finish_two(i, n, edge):
-            finish(i, n, edge)
-            finish(i + 1, n, edge)
-
-        if lv == DEGREE - 1:
-            for ch in range(CH_OUT):
-                n, edge = (1, 0) if 2 * ch < CH_OUT else (2, 3)
-                for i in range(PART_OUT):
-                    finish(PART_OUT * ch + i, n, edge)
-                send_out(ch)
-        else:
-            loop(0, 3, lambda i: finish_two(6 + 2 * i, 2, 3))
-            upward = send_halo(lv + 1, 0)
-            loop(0, 3, lambda i: finish_two(2 * i, 1, 0))
-            halo_in = [upward, send_halo(lv + 1, 1)]
+        def spread_both(i):
+            spread(i, 1, 0)
+            spread(6 + i, 2, 3)
+
+        loop(0, 6, spread_both, 6)
+
+        halo_in[0].wait_recv()
+        halo_rest[0].wait_recv()
+        for i in range(6):
+            low = HALFW[i + 1] * halo_r[lv, 0, 5]
+            for r in range(i + 2, 7):
+                low = low + HALFW[r] * halo_r[lv, 0, 6 + i - r]
+            low = scale * low
+            fix[i] = low
+            if lv + 1 < DEGREE:
+                halo_s[lv + 1, 1, i] = halo_s[lv + 1, 1, i] + low
+        if lv + 1 < DEGREE:
+            downward = send_halo(lv + 1, 1, 0)
+        halo_in[1].wait_recv()
+        halo_rest[1].wait_recv()
+        for i in range(6):
+            high = HALFW[6 - i] * halo_r[lv, 1, 0]
+            for r in range(7 - i, 7):
+                high = high + HALFW[r] * halo_r[lv, 1, i + r - 6]
+            high = scale * high
+            fix[6 + i] = high
+            if lv + 1 < DEGREE:
+                halo_s[lv + 1, 0, i] = halo_s[lv + 1, 0, i] + high
+        if lv + 1 < DEGREE:
+            halo_in = [send_halo(lv + 1, 0, 0), downward]
+
+    for ch in range(CH_OUT):
+        for i in range(PART_OUT * ch, PART_OUT * (ch + 1)):
+            for k, moved in enumerate(transpose_blocks(mended(DEGREE % 2, i, 3 * (i // 6)))):
+                x_out[k, i] = moved
+        send_out(ch)
 
     def unpack_out(i):
         parts = [r_out[m, i] for m in range(4)]
@@ -479,7 +503,7 @@
 
     def near(ch):
         fc_in[ch].wait_recv()
-        loop(PART_OUT * ch, PART_OUT * (ch + 1), lambda i: gram_step(0, filt[i], [filt[i], filt_c[i]]))
+        loop(PART_OUT * ch, PART_OUT * (ch + 1), lambda i: gram_step(0, filt[i], [filt[i], filt_c[i]]), PART_OUT)
 
     def pass_on(ch):
         x_recv[ch].wait_recv()
@@ -493,7 +517,7 @@
         back_own[ch].wait()
         for cp in back_in[ch]:
             cp.wait_recv()
-        loop(PART_OUT * ch, PART_OUT * (ch + 1), unpack_out)
+        loop(PART_OUT * ch, PART_OUT * (ch + 1), unpack_out, PART_OUT)
         planes = pl.ds(PART_OUT * ch, PART_OUT)
         x_recv.append(rcopy(filt.at[planes, give], xr.at[planes], xs_s.at[ch], xs_r.at[ch], across))
         fc_in.append(rcopy(filt.at[planes], filt_c.at[planes], fc_s.at[ch], fc_r.at[ch], core))
@@ -575,13 +599,13 @@
         f(2, 6, NPROJ, ROWS), h(CX, ROWS, ROWS), h(CX, ROWS, ROWS), h(CX, ROWS, ROWS), h(CX, ROWS, ROWS),
         f(CX, ROWS, ORB), f(2, 24, ROWS, ORB), f(ROWS, 2 * ORB), h(6, 2, ROWS, 2 * ORB),
         f(DEGREE, 2, 6, QR, ORB), f(DEGREE, 2, 6, QR, ORB), f(3, 128, ORB),
-        f(DEGREE, 3, NPROJ, ORB), f(DEGREE, 2, 3, NPROJ, ORB), h(3, 128, ORB), h(3, 128, ORB), f(CX, QR, ORB),
+        f(DEGREE, 5, NPROJ, ORB), f(DEGREE, 2, NPROJ, ORB), h(3, 128, ORB), h(3, 128, ORB), f(CX, QR, ORB),
         f(4, CX, QR, ORB), f(4, CX, QR, ORB), f(CX, ROWS, ORB), f(CX, ROWS, ORB), f(CX, 128, ORB), f(CX, 128, ORB),
         f(4, 128, 128), f(2, 7, 2, 16, 128), f(4, 16, 128), f(3, 4, 16, 128), f(4, 16, 128), f(4, 16, 128),
         f(4, 16, 128), f(4, 128, 128),
         dma((3, CH_IN)), dma((3, CH_IN)), dma((3,)), dma((3,)), dma((3,)), dma((3,)), dma((2, 3)), dma((2, 3)),
         dma((3,)), dma((3,)),
-        dma((2,)), dma((2,)), dma((DEGREE, 2)), dma((DEGREE, 2)), dma((DEGREE, 2)), dma((DEGREE, 2)),
+        dma((2,)), dma((2,)), dma((DEGREE, 2, 2)), dma((DEGREE, 2, 2)), dma((DEGREE, 2)), dma((DEGREE, 2)),
         dma((3, CH_OUT)), dma((3, CH_OUT)), dma((CH_OUT,)), dma((CH_OUT,)),
         dma((CH_OUT,)), dma((CH_OUT,)), dma((CH_OUT,)), dma((CH_OUT,)),
         dma, dma, dma, dma, dma((3,)), dma((3,)), dma((5,)), dma((5,)), dma, dma, dma((16,)), dma((CH_OUT,)),

time: 129 us -> 126 us (0.977)
  Pallas kernels: 124 us -> 121 us
    pallas_call x1, Pallas kernels: 124 us -> 121 us  [run(): pl.pallas_call(kernel, out_shape=(jax.ShapeDtypeStruct((CX, ROWS, ORB), F...]
where the time goes in v4:
time: 126 us; the launch traced here: 125 us
  Pallas kernels  121 us (96%)
  local copies, waits for them, and re-layouts  3.4 us (3%)
    pallas_call x1, Pallas kernels, run(): pl.pallas_call(kernel, out_shape=(jax.ShapeDtypeStruct((CX, ROWS, ORB), F...  121 us
    unnamed x4, local copies, waits for them, and re-layouts  3.4 us

profile of v4, /device:TPU:2, one launch (start us, length us, event | category | flops | bytes accessed | tf_op | source)
XLA Modules:
  0.0 124.9 jit_solution(11012146849620963056)
XLA Ops:
  0.6 120.9 %chebyshev.1 = (f32[12,256,128]{2,1,0:T(8,128)}, f32[128,512]{1,0:T(8,128)}) custom-call(f32[12,256,128]{2,1,0:T(8,128)} %bitcast.5, f32[12,16,16]{2,1,0:T(8,128)} %pot.1, f32[52,8,256]{2,1,0:T(8,128)} %bitcast.7, s32[4,13]{1,0:T(4,128)} %planes_ref.1, f32[8]{0:T(128)} %kb.1, bf16[2,256,256]{2,1,0:T(8,128)(2,1)} %constant.2.clone.lap), custom_call_target="tpu_custom_call" | custom-call | tf_op jit(solution)/shard_map/chebyshev/pallas_call | solution.py:615
  121.5 0.0 copy-start
  121.5 2.7 %copy.10 = f32[12,16,16,128]{3,2,1,0:T(8,128)} copy(f32[12,16,16,128]{3,2,1,0:T(8,128)} %bitcast.6) | data formatting | bytes 3145728
  124.2 0.0 copy-done
  124.2 0.7 copy.11
Async XLA Ops:
  121.5 2.7 %copy-start = (f32[128,512]{1,0:T(8,128)S(1)}, f32[128,512]{1,0:T(8,128)}, u32[]{:S(2)}) copy-start(f32[128,512]{1,0:T(8,128)} %get-tuple-element.9) | copy-start | bytes 786436

commit v5 on v4

--- a/solution.py
+++ b/solution.py
@@ -628,12 +628,43 @@
     )(orb, pot, proj, planes_ref, kb, lap)
 
 
+def place_kernel(a, b, a_out, b_out, a_here, b_here, in_sems, out_sems):
+    parts = [(a.at[pl.ds(2 * n, 2)], a_here.at[pl.ds(2 * n, 2)], a_out.at[pl.ds(2 * n, 2)]) for n in range(6)]
+    parts.append((b, b_here, b_out))
+    reads = [pltpu.make_async_copy(src, here, in_sems.at[n]) for n, (src, here, _) in enumerate(parts)]
+    writes = [pltpu.make_async_copy(here, dst, out_sems.at[n]) for n, (_, here, dst) in enumerate(parts)]
+    for cp in reads:
+        cp.start()
+    for read, write in zip(reads, writes):
+        read.wait()
+        write.start()
+    for cp in writes:
+        cp.wait()
+
+
+def place_results(a, b):
+    spec = pl.BlockSpec(memory_space=pl.ANY)
+    return pl.pallas_call(
+        place_kernel,
+        out_shape=(jax.ShapeDtypeStruct(a.shape, F32), jax.ShapeDtypeStruct(b.shape, F32)),
+        in_specs=[spec] * 2,
+        out_specs=(spec, spec),
+        scratch_shapes=[
+            pltpu.VMEM(a.shape, F32), pltpu.VMEM(b.shape, F32),
+            pltpu.SemaphoreType.DMA((7,)), pltpu.SemaphoreType.DMA((7,)),
+        ],
+        compiler_params=pltpu.CompilerParams(vmem_limit_bytes=60 * 2**20),
+        name="place",
+    )(a, b)
+
+
 def shards(orbitals, potential, projectors, atom_planes, kb_energy):
     filtered, gram = run(
         orbitals.reshape(CX, ROWS, ORB), potential, projectors.transpose(0, 2, 1, 3).reshape(52, 8, ROWS),
         atom_planes, kb_energy,
         jnp.asarray(plane_laplacian()),
     )
+    filtered, gram = place_results(filtered, gram)
     return filtered.reshape(orbitals.shape), gram
 
 

time: 126 us -> 125 us (level)
  local copies, waits for them, and re-layouts: 3.4 us -> 0 us
  Pallas kernels: 121 us -> 123 us
    unnamed x4 -> x0, local copies, waits for them, and re-layouts: 3.4 us -> none
    pallas_call x0 -> x1, Pallas kernels: none -> 2.29 us  [place_results(): pl.pallas_call(place_kernel, out_shape=(jax.ShapeDtypeStruct(a.shape, F32...]
where the time goes in v5:
time: 125 us; the launch traced here: 124 us
  Pallas kernels  123 us (98%)
    pallas_call x1, Pallas kernels, run(): pl.pallas_call(kernel, out_shape=(jax.ShapeDtypeStruct((CX, ROWS, ORB), F...  121 us

profile of v5, /device:TPU:2, one launch (start us, length us, event | category | flops | bytes accessed | tf_op | source)
XLA Modules:
  0.0 123.9 jit_solution(4166286563042803260)
XLA Ops:
  0.6 120.9 %chebyshev.1 = (f32[12,256,128]{2,1,0:T(8,128)}, f32[128,512]{1,0:T(8,128)}) custom-call(f32[12,256,128]{2,1,0:T(8,128)} %bitcast.5, f32[12,16,16]{2,1,0:T(8,128)} %pot.1, f32[52,8,256]{2,1,0:T(8,128)} %bitcast.6, s32[4,13]{1,0:T(4,128)} %planes_ref.1, f32[8]{0:T(128)} %kb.1, bf16[2,256,256]{2,1,0:T(8,128)(2,1)} %constant.2.clone.lap), custom_call_target="tpu_custom_call" | custom-call | tf_op jit(solution)/shard_map/chebyshev/pallas_call | solution.py:615
  121.5 2.3 %place.1 = (f32[12,256,128]{2,1,0:T(8,128)}, f32[128,512]{1,0:T(8,128)}) custom-call(f32[12,256,128]{2,1,0:T(8,128)} %get-tuple-element.6.a, f32[128,512]{1,0:T(8,128)} %get-tuple-element.7.b), custom_call_target="tpu_custom_call" | custom-call | tf_op jit(solution)/shard_map/place/pallas_call | solution.py:647
